TPU v7x, 32 devices: a whole 2x2x4 slice. The times are simulated.
32 devices in a mesh: gz: 2 (over x), gx: 4 (over z), gy: 4 (over y, core).
Axes of the slice: x: 2, y: 2, z: 4, core: 2. Of those that a mesh axis runs over, the one named last changes fastest.
Arguments:
- section_pixels: bfloat16 [2, 2048, 8192], P('gz', 'gy', 'gx'), may hold values from -6 to 6
- tissue: int32 [2, 64, 256], P('gz', 'gy', 'gx'), may hold values 0 or 1
- peak_offsets: int32 [2, 2, 64, 256], P(None, 'gz', 'gy', 'gx'), may hold values from -8 to 8
Outputs:
- relaxed: float32 [2, 2, 64, 256], P(None, 'gz', 'gy', 'gx')
- placed: float32 [2, 2, 64, 256], P(None, 'gz', 'gy', 'gx')
All inputs are finite; a program needn't handle non-finite values. No bound on the sum of `tissue` on one device may be relied on, other than what follows from the above.
Results may differ from a plain program's by a relative error of at most 0.0003.
Values may be sent and summed in bfloat16 or wider, within the bound.
A program may use at most 128 MiB of HBM per device.

v0:
```python
import math

import jax
import jax.numpy as jnp
from jax import lax
from jax.sharding import PartitionSpec as P

PATCH = 64
REACH = 12
SPACING = 32
ITERS = 3


sharpness = 32.0
tiny_energy = 1e-06


def from_behind(value, axis, steps):
    count = lax.axis_size(axis)
    initial, last = (max(0, -steps), min(count, count - steps))
    return lax.ppermute(value, axis, [(source, source + steps) for source in range(initial, last)])


def with_halo(shard, sides, width):
    for axis, dim in sides:
        count, length = (lax.axis_size(axis), shard.shape[dim])
        up = [(i, (i + 1) % count) for i in range(count - 1)]
        down = [(j, i) for i, j in up]
        last = lax.slice_in_dim(shard, length - width, length, axis=dim)
        initial = lax.slice_in_dim(shard, 0, width, axis=dim)
        before = lax.ppermute(last, axis, up)
        after = lax.ppermute(initial, axis, down)
        shard = jnp.concatenate([before, shard, after], axis=dim)
    return shard


def prefix(part, axis, combine, identity):
    place = lax.axis_index(axis)
    gathered = lax.all_gather(part, axis)
    state = jnp.zeros_like(part) + jnp.asarray(identity, part.dtype)

    def one(turn, state):
        return combine(state, lax.dynamic_index_in_dim(gathered, turn, 0, False))

    return lax.fori_loop(0, place, one, state)


def phase_tables(length):
    frequency = jnp.arange(length, dtype=jnp.int32)
    angles = jnp.mod(frequency[:, None] * frequency[None, :], length).astype(jnp.float32) * (
        2.0 * math.pi / length
    )
    cosine = jnp.cos(angles)
    sine_part = jnp.sin(angles)
    first_table = jnp.concatenate([cosine, -sine_part], 0).astype(jnp.bfloat16)
    second_table = jnp.stack(
        [jnp.stack([cosine, sine_part], 0), jnp.stack([-sine_part, cosine], 0)], 0
    ).astype(jnp.bfloat16)
    return (first_table, second_table)


def transform_window(section, block_rows, node_cols, first_table, second_table):
    width_padded = section.shape[1]
    blocks = section.reshape(block_rows + 1, SPACING, width_padded)
    upper = jnp.einsum(
        "fr,brw->fbw", first_table[:, :SPACING], blocks[:-1], preferred_element_type=jnp.float32
    )
    lower = jnp.einsum(
        "fr,brw->fbw", first_table[:, SPACING:], blocks[1:], preferred_element_type=jnp.float32
    )
    half_spec = (upper + lower).astype(jnp.bfloat16)
    half_spec = half_spec.reshape(2, PATCH, block_rows, node_cols + 1, SPACING)
    left = jnp.einsum(
        "okgc,kfijc->ogfij",
        second_table[..., :SPACING],
        half_spec[:, :, :, :-1, :],
        preferred_element_type=jnp.float32,
    )
    right = jnp.einsum(
        "okgc,kfijc->ogfij",
        second_table[..., SPACING:],
        half_spec[:, :, :, 1:, :],
        preferred_element_type=jnp.float32,
    )
    spec = (left + right).reshape(2, PATCH, PATCH, block_rows * node_cols)
    squares_field = jnp.square(section.astype(jnp.float32)).reshape(
        block_rows + 1, SPACING, node_cols + 1, SPACING
    )
    block_energy = jnp.sum(squares_field, axis=(1, 3))
    energy = (
        block_energy[:-1, :-1]
        + block_energy[1:, :-1]
        + block_energy[:-1, 1:]
        + block_energy[1:, 1:]
    )
    return (spec, energy.reshape(block_rows * node_cols))


def phase_of(values):
    frequency = jnp.arange(PATCH, dtype=jnp.int32).reshape((PATCH,) + (1,) * values.ndim)
    angles = jnp.mod(frequency * values[None], PATCH).astype(jnp.float32) * (2.0 * math.pi / PATCH)
    return (jnp.cos(angles), jnp.sin(angles))


def match_patches(spec_a, energy_a, spec_b, energy_b, offset_pair, living):
    highest = lax.Precision.HIGHEST
    cross_real = spec_a[0] * spec_b[0] + spec_a[1] * spec_b[1]
    cross_imag = spec_a[0] * spec_b[1] - spec_a[1] * spec_b[0]
    row_cos, row_sin = phase_of(offset_pair[0])
    col_cos, col_sin = phase_of(offset_pair[1])
    turn_cosine = col_cos[:, None, :] * row_cos[None] - col_sin[:, None, :] * row_sin[None]
    turn_sine = col_cos[:, None, :] * row_sin[None] + col_sin[:, None, :] * row_cos[None]
    rotated = jnp.stack(
        [
            cross_real * turn_cosine - cross_imag * turn_sine,
            cross_real * turn_sine + cross_imag * turn_cosine,
        ],
        0,
    )
    lag_count = 2 * REACH + 1
    lag_values = jnp.arange(lag_count, dtype=jnp.int32) - REACH
    lag_cos, lag_sin = phase_of(lag_values)
    row_lag_table = jnp.stack(
        [jnp.stack([lag_cos, -lag_sin], 0), jnp.stack([lag_sin, lag_cos], 0)], 0
    )
    col_lag_table = jnp.stack([lag_cos, -lag_sin], 0)
    first_pass = jnp.einsum("kgfp,jkfe->jegp", rotated, row_lag_table, precision=highest)
    correlation = jnp.einsum("jegp,jgh->ehp", first_pass, col_lag_table, precision=highest) / float(
        PATCH * PATCH
    )
    likeness = correlation / jnp.sqrt(energy_a * energy_b + tiny_energy)
    weights = jnp.exp(sharpness * likeness)
    weight_sum = jnp.sum(weights, axis=(0, 1))
    lag_steps = lag_values.astype(jnp.float32)
    row_shift = jnp.sum(weights * lag_steps[:, None, None], axis=(0, 1)) / weight_sum
    col_shift = jnp.sum(weights * lag_steps[None, :, None], axis=(0, 1)) / weight_sum
    target = jnp.stack(
        [
            offset_pair[0].astype(jnp.float32) + row_shift,
            offset_pair[1].astype(jnp.float32) + col_shift,
        ],
        0,
    )
    stiffness = living * weight_sum / float(lag_count * lag_count)
    return (target, stiffness)


def neighbour_sum(padded):
    return (
        padded[..., :-2, 1:-1]
        + padded[..., 2:, 1:-1]
        + padded[..., 1:-1, :-2]
        + padded[..., 1:-1, 2:]
    )


def relax_update(moved, living, stiffness, target, living_padded, moved_padded):
    neighbours = neighbour_sum(living_padded)
    pulled = neighbour_sum(living_padded[None] * moved_padded)
    numerator = moved + stiffness[None] * target + living[None] * pulled
    return numerator / (1.0 + stiffness + living * neighbours)[None]


def add_fields(earlier, later):
    return earlier + later


def shards(section_pixels, tissue, peak_offsets):
    sections, pixel_rows, pixel_cols = section_pixels.shape
    node_rows = pixel_rows // SPACING
    node_cols = pixel_cols // SPACING
    margin = SPACING // 2
    following = from_behind(section_pixels[0], "gz", -1)
    joined = jnp.concatenate([section_pixels, following[None]], 0)
    padded = with_halo(joined, (("gx", 2), ("gy", 1)), margin)
    block_rows = math.gcd(node_rows, max(1, 128 // node_cols))
    block_count = node_rows // block_rows
    block_size = block_rows * node_cols
    first_table, second_table = phase_tables(PATCH)
    living = tissue.astype(jnp.float32)
    offset_blocks = jnp.transpose(
        peak_offsets.reshape(2, sections, block_count, block_size), (2, 0, 1, 3)
    )
    living_blocks = jnp.transpose(living.reshape(sections, block_count, block_size), (1, 0, 2))

    def block_match(inputs):
        position, offset_block, living_block = inputs
        window = lax.dynamic_slice_in_dim(
            padded, position * (block_rows * SPACING), block_rows * SPACING + SPACING, 1
        )
        previous = transform_window(window[0], block_rows, node_cols, first_table, second_table)
        current = transform_window(window[1], block_rows, node_cols, first_table, second_table)
        target, stiffness = match_patches(
            previous[0], previous[1], current[0], current[1], offset_block[:, 0], living_block[0]
        )
        targets = [target]
        stiffs = [stiffness]
        return (jnp.stack(targets, 1), jnp.stack(stiffs, 0))

    positions = jnp.arange(block_count, dtype=jnp.int32)
    target_blocks, stiff_blocks = lax.map(block_match, (positions, offset_blocks, living_blocks))
    target = jnp.transpose(target_blocks, (1, 2, 0, 3)).reshape(2, sections, node_rows, node_cols)
    stiffness = jnp.transpose(stiff_blocks, (1, 0, 2)).reshape(sections, node_rows, node_cols)
    moved = living[None] * target
    for sweep_index in range(ITERS):
        payload = jnp.concatenate([living[None], moved], 0)
        extended = with_halo(payload, (("gx", 3), ("gy", 2)), 1)
        moved = relax_update(moved, living, stiffness, target, extended[0], extended[1:])
    running = jnp.cumsum(moved, axis=1)
    slab_total = running[:, -1]
    before = prefix(slab_total, "gz", add_fields, jnp.zeros_like(slab_total))
    placed = running + before[:, None]
    return (moved, placed)


def solution(mesh):
    placed = (P("gz", "gy", "gx"), P("gz", "gy", "gx"), P(None, "gz", "gy", "gx"))
    return jax.shard_map(
        shards,
        mesh=mesh,
        in_specs=placed,
        out_specs=(P(None, "gz", "gy", "gx"), P(None, "gz", "gy", "gx")),
        check_vma=False,
    )
```

profile of v0, /device:TPU:1, one launch (start us, length us, event | category | flops | bytes accessed | tf_op | source)
XLA Modules:
  0.0 960.2 jit_solution(3522406973297203717)
XLA Ops:
  3.7 45.9 %collective-permute-done = bf16[512,2048]{1,0:T(8,128)(2,1)S(1)} collective-permute-done((bf16[512,2048]{1,0:T(8,128)(2,1)}, bf16[512,2048]{1,0:T(8,128)(2,1)S(1)}, u32[]{:S(2)}, u32[]{:S(2)}) %collective-permute-start) | collective-permute-done | bytes 2097184 | tf_op jit(solution)/shard_map/ppermute | solution.py:21
  62.4 9.1 concatenate.41
  89.2 806.0 %while.24 = (s32[]{:T(128)}, f32[8,2,1,128]{3,1,2,0:T(2,128)}, f32[8,1,128]{2,1,0:T(1,128)}, s32[8,2,1,128]{3,0,1,2:T(8,128)}, s32[8]{0:T(128)}, /*index=5*/bf16...) while((s32[]{:T(128)}, f32[8,2,1,128]{3,1,2,0:T(2,128)}, ...), condition=%wide.region_6.7_spmd, body=%wide.region_0.6_spmd.sunk | while | flops 1442033280 | bytes 114443120 | solution.py:201
  100.4 6.0 copy.76
  110.9 6.0 copy.77
  116.9 7.9 fusion.207
  132.5 6.0 copy.74
  143.1 6.0 copy.75
  153.7 6.5 multiply_add_fusion.4
  201.1 6.0 copy.76
  217.6 7.9 fusion.207
  254.5 6.5 multiply_add_fusion.4
  318.4 7.9 fusion.207
  355.2 6.5 multiply_add_fusion.4
  419.2 7.9 fusion.207
  456.0 6.5 multiply_add_fusion.4
  520.0 7.9 fusion.207
  556.8 6.5 multiply_add_fusion.4
  620.7 7.9 fusion.207
  657.5 6.5 multiply_add_fusion.4
  721.4 7.9 fusion.207
  758.3 6.5 multiply_add_fusion.4
  822.1 7.9 fusion.207
  859.0 6.5 multiply_add_fusion.4
  (509 shorter events, 751.9 us)
Async XLA Ops:
  0.6 49.0 %collective-permute-start = (bf16[512,2048]{1,0:T(8,128)(2,1)}, bf16[512,2048]{1,0:T(8,128)(2,1)S(1)}, u32[]{:S(2)}, u32[]{:S(2)}) collective-permute-start(bf16[512,2048]{1,0:T(8,128)(2,1)} %bitcast.270), channel_id=1, source_target_pairs={{16,0},{17,1},{18,2},{19,3},{20,4},{21,5},{22,6},{23,7},{24,8},{25... | collective-permute-start | bytes 6291464 | tf_op jit(solution)/shard_map/ppermute | solution.py:21
  50.9 7.7 collective-permute-start.1
  54.6 7.9 collective-permute-start.2
  72.6 9.1 collective-permute-start.3
  78.3 6.4 collective-permute-start.4
  89.2 59.8 %copy-start.2 = (bf16[2,2,64,64]{2,3,1,0:T(8,128)(2,1)}, bf16[2,2,64,64]{2,3,1,0:T(8,128)(2,1)S(1)}, u32[]{:S(2)}) copy-start(bf16[2,2,64,64]{2,3,1,0:T(8,128)(2,1)S(1)} %get-tuple-element.442) | copy-start | bytes 98308 | tf_op jit(solution)/shard_map/while
  190.0 59.9 %copy-start.2 = (bf16[2,2,64,64]{2,3,1,0:T(8,128)(2,1)}, bf16[2,2,64,64]{2,3,1,0:T(8,128)(2,1)S(1)}, u32[]{:S(2)}) copy-start(bf16[2,2,64,64]{2,3,1,0:T(8,128)(2,1)S(1)} %get-tuple-element.442) | copy-start | bytes 98308 | tf_op jit(solution)/shard_map/while
  290.7 59.8 %copy-start.2 = (bf16[2,2,64,64]{2,3,1,0:T(8,128)(2,1)}, bf16[2,2,64,64]{2,3,1,0:T(8,128)(2,1)S(1)}, u32[]{:S(2)}) copy-start(bf16[2,2,64,64]{2,3,1,0:T(8,128)(2,1)S(1)} %get-tuple-element.442) | copy-start | bytes 98308 | tf_op jit(solution)/shard_map/while
  391.5 59.8 %copy-start.2 = (bf16[2,2,64,64]{2,3,1,0:T(8,128)(2,1)}, bf16[2,2,64,64]{2,3,1,0:T(8,128)(2,1)S(1)}, u32[]{:S(2)}) copy-start(bf16[2,2,64,64]{2,3,1,0:T(8,128)(2,1)S(1)} %get-tuple-element.442) | copy-start | bytes 98308 | tf_op jit(solution)/shard_map/while
  492.3 59.8 %copy-start.2 = (bf16[2,2,64,64]{2,3,1,0:T(8,128)(2,1)}, bf16[2,2,64,64]{2,3,1,0:T(8,128)(2,1)S(1)}, u32[]{:S(2)}) copy-start(bf16[2,2,64,64]{2,3,1,0:T(8,128)(2,1)S(1)} %get-tuple-element.442) | copy-start | bytes 98308 | tf_op jit(solution)/shard_map/while
  593.0 59.8 %copy-start.2 = (bf16[2,2,64,64]{2,3,1,0:T(8,128)(2,1)}, bf16[2,2,64,64]{2,3,1,0:T(8,128)(2,1)S(1)}, u32[]{:S(2)}) copy-start(bf16[2,2,64,64]{2,3,1,0:T(8,128)(2,1)S(1)} %get-tuple-element.442) | copy-start | bytes 98308 | tf_op jit(solution)/shard_map/while
  693.7 59.8 %copy-start.2 = (bf16[2,2,64,64]{2,3,1,0:T(8,128)(2,1)}, bf16[2,2,64,64]{2,3,1,0:T(8,128)(2,1)S(1)}, u32[]{:S(2)}) copy-start(bf16[2,2,64,64]{2,3,1,0:T(8,128)(2,1)S(1)} %get-tuple-element.442) | copy-start | bytes 98308 | tf_op jit(solution)/shard_map/while
  897.5 4.5 collective-permute-start.5
  900.7 4.6 collective-permute-start.6
  906.1 7.2 collective-permute-start.7
  909.3 4.9 collective-permute-start.8
  917.4 5.3 collective-permute-start.10
  918.7 4.9 collective-permute-start.9
  924.4 5.8 collective-permute-start.11
  928.2 4.9 collective-permute-start.12
  936.3 5.2 collective-permute-start.13
  940.3 4.6 collective-permute-start.14
  945.6 5.3 collective-permute-start.15
  949.0 4.9 collective-permute-start.16
  (52 other events, 268.5 us)
where the time goes:
time: 968 us; the launch traced here: 960 us
  local copies, waits for them, and re-layouts  435 us (45%)
  matrix products  246 us (25%)
  other arithmetic  155 us (16%)
  waiting for transfers between devices  67.4 us (7%)
  starting transfers between devices  45.1 us (5%)
    while x144, local copies, waits for them, and re-layouts  195 us
    dot_general x16, matrix products, transform_window(): jnp.einsum('okgc,kfijc->ogfij', second_table[..., SPACING:], half_spec[:,...  101 us
    slice x16, local copies, waits for them, and re-layouts, transform_window(): half_spec[:, :, :, 1:, :]  85.6 us
    dot_general x16, matrix products, transform_window(): jnp.einsum('okgc,kfijc->ogfij', second_table[..., :SPACING], half_spec[:,...  72.9 us
    add x8, other arithmetic, match_patches(): cross_real = spec_a[0] * spec_b[0] + spec_a[1] * spec_b[1]  52.2 us
    ppermute x1, waiting for transfers between devices, from_behind(): lax.ppermute(value, axis, [(source, source + steps) for source in range(i...  45.9 us
    add x8, local copies, waits for them, and re-layouts, match_patches(): cross_real = spec_a[0] * spec_b[0] + spec_a[1] * spec_b[1]  33.6 us
    square x16, local copies, waits for them, and re-layouts, transform_window(): jnp.square(section.astype(jnp.float32))  31.8 us
  transfers between devices with their start and end apart: 17, of which 10 were waited for; matrix products, arithmetic and copies ran while one was open for 1% of the time, Pallas kernels for 0%

commit v1 on v0

v1 whole, which is shorter than its diff:
```python
import functools
import math

import jax
import jax.numpy as jnp
import ml_dtypes
import numpy as np
from jax import lax
from jax.experimental import pallas as pl
from jax.experimental.pallas import tpu as pltpu
from jax.sharding import PartitionSpec as P

PATCH = 64
REACH = 12
SPACING = 32
ITERS = 3
BOUND = 8
FAR = BOUND + REACH
LAG_ROWS = 48
HALF = PATCH // 2

sharpness = 32.0
tiny_energy = 1e-06


def bf16(table):
    return np.asarray(table, np.float32).astype(ml_dtypes.bfloat16)


def split(table):
    high = bf16(table)
    return high, bf16(np.asarray(table, np.float32) - high.astype(np.float32))


@functools.lru_cache(None)
def tables():
    n = np.arange(PATCH)
    angle = 2.0 * math.pi * ((n[:, None] * n[None, :]) % PATCH) / PATCH
    cosine, sine = np.cos(angle), np.sin(angle)
    row_table = np.zeros((80, PATCH))
    row_table[:HALF] = cosine[:HALF]
    row_table[HALF:PATCH] = -sine[:HALF]
    row_table[PATCH] = cosine[HALF]
    second = np.zeros((2, 256, 2, 2, 2, PATCH))
    spread = np.zeros((256, 4, PATCH))
    for pair in range(2):
        for q in range(2):
            node = 2 * pair + q
            rows = slice(SPACING * node, SPACING * node + PATCH)
            second[0, rows, pair, 0, q] = cosine.T
            second[0, rows, pair, 1, q] = -sine.T
            second[1, rows, pair, 0, q] = sine.T
            second[1, rows, pair, 1, q] = cosine.T
            spread[rows, node] = 1.0
    lags = np.arange(2 * FAR + 1) - FAR
    lag_angle = 2.0 * math.pi * ((n[:, None] * lags[None, :]) % PATCH) / PATCH
    lag_cos, lag_sin = np.cos(lag_angle), np.sin(lag_angle)
    back = np.zeros((2, 2, PATCH, 2, 2, PATCH))
    for q in range(2):
        back[0, q, :, 0, q, : lags.size] = lag_cos
        back[1, q, :, 0, q, : lags.size] = -lag_sin
        back[0, q, :, 1, q, : lags.size] = lag_sin
        back[1, q, :, 1, q, : lags.size] = lag_cos
    back_high, back_low = split(back.reshape(256, 256))
    fold = np.where(np.arange(HALF) == 0, 1.0, 2.0)[None]
    rows = np.zeros((LAG_ROWS, 2 * HALF))
    rows[: lags.size, :HALF] = fold * lag_cos[:HALF].T
    rows[: lags.size, HALF:] = -fold * lag_sin[:HALF].T
    row_high, row_low = split(rows)
    row_back = np.concatenate([row_high, row_high, row_low], 1)
    gather = np.zeros((2, 4, PATCH, 128))
    lane_lag = np.arange(PATCH) - FAR
    for node in range(4):
        gather[0, node, :, node] = 1.0
        gather[0, node, :, 4 + node] = lane_lag
        gather[1, node, :, 8 + node] = 1.0
    return (
        bf16(row_table),
        bf16(second.reshape(2, 256, 512)),
        np.asarray(spread.reshape(256, 256), np.float32),
        back_high,
        back_low,
        row_back,
        np.asarray(gather.reshape(2, 256, 128), np.float32),
    )


def match_kernel(
    node_rows,
    sign_ref,
    mine_ref,
    theirs_ref,
    offsets_ref,
    row_ref,
    second_ref,
    spread_ref,
    back_high_ref,
    back_low_ref,
    row_back_ref,
    gather_ref,
    out_ref,
    half_ref,
    nyquist_ref,
    squares_ref,
):
    f32, b16 = jnp.float32, jnp.bfloat16
    step = pl.program_id(0)

    def dot(a, b):
        return jnp.dot(a, b, preferred_element_type=f32)

    def exact(a, b):
        return jnp.dot(a, b, preferred_element_type=f32, precision=lax.Precision.HIGHEST)

    @pl.when(step == 0)
    def _():
        def one(i, _):
            for which, image in enumerate((mine_ref, theirs_ref)):
                rows = image[pl.ds(pl.multiple_of(i * SPACING, SPACING), PATCH), :]
                got = dot(row_ref[...], rows)
                at = pl.ds(pl.multiple_of(i * HALF, HALF), HALF)
                half_ref[which, 0, at, :] = got[:HALF].astype(b16)
                half_ref[which, 1, at, :] = got[HALF:PATCH].astype(b16)
                nyquist_ref[which, pl.ds(i, 1), :] = got[PATCH : PATCH + 1].astype(b16).astype(f32)
                wide = rows.astype(f32)
                squares_ref[which, pl.ds(i, 1), :] = jnp.sum(wide * wide, axis=0, keepdims=True)
            return 0

        lax.fori_loop(0, node_rows, one, 0)

    lanes = pl.ds(pl.multiple_of(step * 128, 128), 256)
    sign = sign_ref[0]
    spectra, edges, energies = [], [], []
    for which in range(2):
        spectra.append(
            dot(half_ref[which, 0, :, lanes], second_ref[0])
            + dot(half_ref[which, 1, :, lanes], second_ref[1])
        )
        edges.append(dot(nyquist_ref[which, :, lanes].astype(b16), second_ref[0]))
        energies.append(exact(squares_ref[which, :, lanes], spread_ref[...]))
    scale = (sharpness / (PATCH * PATCH)) / jnp.sqrt(energies[0] * energies[1] + tiny_energy)

    def over_columns(first, then, pair):
        real, imag = slice(256 * pair, 256 * pair + 128), slice(256 * pair + 128, 256 * pair + 256)
        cross_real = first[:, real] * then[:, real] + first[:, imag] * then[:, imag]
        cross_imag = sign * (first[:, real] * then[:, imag] - first[:, imag] * then[:, real])
        cross = jnp.concatenate([cross_real, cross_imag], 1)
        high = cross.astype(b16)
        low = (cross - high.astype(f32)).astype(b16)
        return dot(high, back_high_ref[...]) + dot(low, back_high_ref[...]) + dot(high, back_low_ref[...])

    columns = [over_columns(spectra[0], spectra[1], pair) for pair in range(2)]
    edge_columns = jnp.concatenate(
        [over_columns(edges[0], edges[1], pair)[:, :128] for pair in range(2)], 1
    )
    row_lag = lax.broadcasted_iota(jnp.int32, (LAG_ROWS, 256), 0) - FAR
    col_lag = (lax.broadcasted_iota(jnp.int32, (LAG_ROWS, 256), 1) & (PATCH - 1)) - FAR
    alternate = jnp.where((row_lag & 1) == 0, 1.0, -1.0).astype(f32)
    row_lag = row_lag.astype(f32)
    col_lag = col_lag.astype(f32)
    totals, row_totals = [], []
    for i in range(node_rows):
        rows = slice(i * HALF, (i + 1) * HALF)
        field = jnp.concatenate(
            [
                jnp.concatenate([columns[0][rows, :128], columns[1][rows, :128]], 1),
                jnp.concatenate([columns[0][rows, 128:], columns[1][rows, 128:]], 1),
            ],
            0,
        )
        high = field.astype(b16)
        low = (field - high.astype(f32)).astype(b16)
        found = dot(row_back_ref[...], jnp.concatenate([high, low, high], 0))
        found = found + alternate * edge_columns[i : i + 1]
        inside = (jnp.abs(row_lag - offsets_ref[0, i : i + 1, :]) <= REACH) & (
            jnp.abs(col_lag - offsets_ref[1, i : i + 1, :]) <= REACH
        )
        weights = jnp.where(inside, jnp.exp(found * scale[i : i + 1]), 0.0)
        totals.append(jnp.sum(weights, axis=0, keepdims=True))
        row_totals.append(jnp.sum(weights * row_lag, axis=0, keepdims=True))
    out_ref[0] = exact(jnp.concatenate(totals, 0), gather_ref[0]) + exact(
        jnp.concatenate(row_totals, 0), gather_ref[1]
    )


def match(mine, theirs, sign, offsets):
    node_rows, node_cols = offsets.shape[1:]
    groups = node_cols // 4
    width = mine.shape[1]
    constants = [jnp.asarray(table) for table in tables()]
    spread_offsets = jnp.repeat(offsets.astype(jnp.float32), PATCH, axis=2)
    whole = lambda a: pl.BlockSpec(a.shape, lambda m, n=a.ndim: (0,) * n)
    out = pl.pallas_call(
        functools.partial(match_kernel, node_rows),
        grid=(groups,),
        out_shape=jax.ShapeDtypeStruct((groups, node_rows, 128), jnp.float32),
        in_specs=[
            pl.BlockSpec(memory_space=pltpu.SMEM),
            whole(mine),
            whole(theirs),
            pl.BlockSpec((2, node_rows, 256), lambda m: (0, 0, m)),
        ]
        + [whole(table) for table in constants],
        out_specs=pl.BlockSpec((1, node_rows, 128), lambda m: (m, 0, 0)),
        scratch_shapes=[
            pltpu.VMEM((2, 2, node_rows * HALF, width), jnp.bfloat16),
            pltpu.VMEM((2, node_rows, width), jnp.float32),
            pltpu.VMEM((2, node_rows, width), jnp.float32),
        ],
        compiler_params=pltpu.CompilerParams(vmem_limit_bytes=56 * 1024 * 1024),
    )(sign, mine, theirs, spread_offsets, *constants)
    sums = jnp.transpose(out[:, :, :12].reshape(groups, node_rows, 3, 4), (2, 1, 0, 3))
    sums = sums.reshape(3, node_rows, node_cols)
    return jnp.stack([sums[2] / sums[0], sums[1] / sums[0], sums[0]], 0)


def beside(value, axis, steps):
    count = lax.axis_size(axis)
    pairs = [(i, i + steps) for i in range(count) if 0 <= i + steps < count]
    return lax.ppermute(value, axis, pairs)


def bordered(field, axis, dim, width):
    length = field.shape[dim]
    before = beside(lax.slice_in_dim(field, length - width, length, axis=dim), axis, 1)
    after = beside(lax.slice_in_dim(field, 0, width, axis=dim), axis, -1)
    return before, after


def neighbour_sum(padded):
    return (
        padded[..., :-2, 1:-1]
        + padded[..., 2:, 1:-1]
        + padded[..., 1:-1, :-2]
        + padded[..., 1:-1, 2:]
    )


def relax(target, stiffness, living):
    fields = jnp.concatenate([target, stiffness[None], living[None]], 0)
    before, after = bordered(fields, "gx", 3, ITERS)
    fields = jnp.concatenate([before, fields, after], 3)
    before, after = bordered(fields, "gy", 2, ITERS)
    fields = jnp.concatenate([before, fields, after], 2)
    target, stiffness, living = fields[:2], fields[2], fields[3]
    moved = living[None] * target
    for _ in range(ITERS):
        pulled = neighbour_sum(living[None] * moved)
        count = neighbour_sum(living)
        inner = (slice(None), slice(1, -1), slice(1, -1))
        target, moved = target[(slice(None),) + inner], moved[(slice(None),) + inner]
        stiffness, living = stiffness[inner], living[inner]
        moved = (moved + stiffness[None] * target + living[None] * pulled) / (
            1.0 + stiffness + living * count
        )[None]
    return moved


def shards(section_pixels, tissue, peak_offsets):
    margin = SPACING // 2
    own = section_pixels[0]
    pixel_rows, pixel_cols = own.shape
    node_rows = pixel_rows // SPACING
    slabs = lax.axis_size("gz")
    place = lax.axis_index("gz")
    before, after = bordered(own, "gx", 1, margin)
    spare = jnp.zeros((pixel_rows, 128 - 2 * margin), own.dtype)
    own = jnp.concatenate([before, own, after, spare], 1)
    before, after = bordered(own, "gy", 0, margin)
    own = jnp.concatenate([before, own, after], 0)
    offsets = peak_offsets[:, 0].astype(jnp.float32)
    living = tissue.astype(jnp.float32)
    per_node = jnp.float32((2 * REACH + 1) ** 2)

    if slabs == 2 and node_rows % 16 == 0:
        half_rows = node_rows // 2
        strip = half_rows * SPACING + SPACING
        swap = [(0, 1), (1, 0)]
        first = place == 0
        theirs = lax.ppermute(
            lax.dynamic_slice_in_dim(own, (1 - place) * (half_rows * SPACING), strip, 0), "gz", swap
        )
        mine = lax.dynamic_slice_in_dim(own, place * (half_rows * SPACING), strip, 0)
        nodes = jnp.concatenate([offsets, living], 0)
        other_nodes = lax.ppermute(nodes, "gz", swap)
        nodes_0 = jnp.where(first, nodes, other_nodes)
        nodes_1 = jnp.where(first, other_nodes, nodes)
        sign = jnp.where(first, 1.0, -1.0).astype(jnp.float32).reshape(1)
        ours = match(
            mine, theirs, sign, lax.dynamic_slice_in_dim(nodes_0[:2], place * half_rows, half_rows, 1)
        )
        others = lax.ppermute(ours, "gz", swap)
        matched = jnp.concatenate(
            [jnp.where(first, ours, others), jnp.where(first, others, ours)], 1
        )
        target = jnp.stack([matched[:2], nodes_1[:2]], 1)
        alive = jnp.stack([nodes_0[2], nodes_1[2]], 0)
        stiffness = jnp.stack([nodes_0[2] * matched[2] / per_node, nodes_1[2]], 0)
        moved = relax(target, stiffness, alive)
        relaxed = jnp.where(first, moved[:, 0], moved[:, 1])
        placed = jnp.where(first, moved[:, 0], moved[:, 0] + moved[:, 1])
        return relaxed[:, None], placed[:, None]

    theirs = beside(own, "gz", -1)
    matched = match(own, theirs, jnp.ones((1,), jnp.float32), offsets)
    moved = relax(matched[:2, None], living * matched[2:] / per_node, living)
    placed = moved
    reach = 1
    while reach < slabs:
        placed = placed + beside(placed, "gz", reach)
        reach *= 2
    return moved, placed


def solution(mesh):
    placed = (P("gz", "gy", "gx"), P("gz", "gy", "gx"), P(None, "gz", "gy", "gx"))
    return jax.shard_map(
        shards,
        mesh=mesh,
        in_specs=placed,
        out_specs=(P(None, "gz", "gy", "gx"), P(None, "gz", "gy", "gx")),
        check_vma=False,
    )
```

time: 968 us -> 113 us (0.12)
  local copies, waits for them, and re-layouts: 435 us -> 10.6 us
  matrix products: 246 us -> 0 us
  other arithmetic: 155 us -> 2.34 us
  Pallas kernels: 0 us -> 30.3 us
  waiting for transfers between devices: 67.4 us -> 42.9 us
  starting transfers between devices: 45.1 us -> 25.4 us
    dot_general x80 -> x0, matrix products: 246 us -> none  [the longest x16 101 us: transform_window(): jnp.einsum('okgc,kfijc->ogfij', second_table[..., SPACING:], half_spec[:,...]
    while x145 -> x0, local copies, waits for them, and re-layouts: 196 us -> none
    slice x28 -> x12, local copies, waits for them, and re-layouts: 103 us -> 2.39 us  [the longest x2 1.08 us: bordered(): after = beside(lax.slice_in_dim(field, 0, width, axis=dim), axis, -1)]
    add x17 -> x0, other arithmetic: 52.8 us -> none  [the longest x8 52.2 us: match_patches(): cross_real = spec_a[0] * spec_b[0] + spec_a[1] * spec_b[1]]
    add x9 -> x0, local copies, waits for them, and re-layouts: 33.7 us -> none  [the longest x8 33.6 us: match_patches(): cross_real = spec_a[0] * spec_b[0] + spec_a[1] * spec_b[1]]
    square x16 -> x0, local copies, waits for them, and re-layouts: 31.8 us -> none  [transform_window(): jnp.square(section.astype(jnp.float32))]
    pallas_call x0 -> x1, Pallas kernels: none -> 30.3 us  [match(): pl.pallas_call(functools.partial(match_kernel, node_rows), grid=(groups,)...]
    sub x8 -> x0, local copies, waits for them, and re-layouts: 28.2 us -> none  [match_patches(): cross_imag = spec_a[0] * spec_b[1] - spec_a[1] * spec_b[0]]
  transfers between devices with their start and end apart: 17 -> 11, of which waited for: 10 -> 8; matrix products, arithmetic and copies ran while one was open for 1% -> 1% of each run, Pallas kernels for 0% -> 0%
where the time goes in v1:
time: 113 us
  waiting for transfers between devices  42.9 us (38%)
  Pallas kernels  30.3 us (27%)
  starting transfers between devices  25.4 us (22%)
  local copies, waits for them, and re-layouts  10.6 us (9%)
  other arithmetic  2.34 us (2%)
    pallas_call x1, Pallas kernels, match(): pl.pallas_call(functools.partial(match_kernel, node_rows), grid=(groups,)...  30.3 us
    ppermute x1, waiting for transfers between devices, shards(): other_nodes = lax.ppermute(nodes, 'gz', swap)  26.2 us
    ppermute x8, starting transfers between devices, beside(): return lax.ppermute(value, axis, pairs)  22.6 us
    ppermute x8, waiting for transfers between devices, beside(): return lax.ppermute(value, axis, pairs)  15.4 us
    concatenate x1, local copies, waits for them, and re-layouts, shards(): own = jnp.concatenate([before, own, after, spare], 1)  4.58 us
  transfers between devices with their start and end apart: 11, of which 8 were waited for; matrix products, arithmetic and copies ran while one was open for 1% of the time, Pallas kernels for 0%

profile of v1, /device:TPU:1, one launch (start us, length us, event | category | flops | bytes accessed | tf_op | source)
XLA Modules:
  0.0 112.6 jit_solution(12934993597739443300)
XLA Ops:
  0.6 1.1 fusion.26
  1.7 4.0 %collective-permute-start = (bf16[512,16]{1,0:T(8,128)(2,1)S(1)}, bf16[512,16]{1,0:T(8,128)(2,1)S(1)}, u32[]{:S(2)}, u32[]{:S(2)}) collective-permute-start(bf16[512,16]{1,0:T(8,128)(2,1)S(1)} %get-tuple-element.17), channel_id=1, source_target_pairs={{0,4},{4,8},{8,12},{1,5},{5,9},{9,13},{2,6},{6,10},{10,14},{3,7},{... | collective-permute-start | bytes 49160 | tf_op jit(solution)/shard_map/ppermute | solution.py:220
  5.8 1.3 %collective-permute-start.1 = (bf16[512,16]{1,0:T(8,128)(2,1)S(1)}, bf16[512,16]{1,0:T(8,128)(2,1)S(1)}, u32[]{:S(2)}, u32[]{:S(2)}) collective-permute-start(bf16[512,16]{1,0:T(8,128)(2,1)S(1)} %get-tuple-element.16), channel_id=1, source_target_pairs={{4,0},{8,4},{12,8},{5,1},{9,5},{13,9},{6,2},{10,6},{14,10},{7,3},{... | collective-permute-start | bytes 49160 | tf_op jit(solution)/shard_map/ppermute | solution.py:220
  7.1 0.8 collective-permute-done
  7.9 3.6 %collective-permute-done.1 = bf16[512,16]{1,0:T(8,128)(2,1)S(1)} collective-permute-done((bf16[512,16]{1,0:T(8,128)(2,1)S(1)}, bf16[512,16]{1,0:T(8,128)(2,1)S(1)}, u32[]{:S(2)}, u32[]{:S(2)}) %collective-permute-start.1) | collective-permute-done | bytes 16416 | tf_op jit(solution)/shard_map/ppermute | solution.py:220
  11.5 4.6 %concatenate.21 = bf16[512,2176]{1,0:T(8,128)(2,1)S(1)} concatenate(bf16[512,16]{1,0:T(8,128)(2,1)S(1)} %collective-permute-done, bf16[512,2048]{1,0:T(8,128)(2,1)} %bitcast.30, bf16[512,16]{1,0:T(8,128)(2,1)S(1)} %collective-permute-done.1, bf16[512,96]{1,0:T(8,128)(2,1)S(1)} %broadcast_in_dim.8), dimensions={1} | concatenate | bytes 4456448 | tf_op jit(solution)/shard_map/concatenate | solution.py:268
  16.1 5.1 %collective-permute-start.2 = (bf16[16,2176]{1,0:T(8,128)(2,1)S(1)}, bf16[16,2176]{1,0:T(8,128)(2,1)S(1)}, u32[]{:S(2)}, u32[]{:S(2)}) collective-permute-start(bf16[16,2176]{1,0:T(8,128)(2,1)S(1)} %get-tuple-element.14), channel_id=1, source_target_pairs={{0,1},{1,2},{2,3},{4,5},{5,6},{6,7},{8,9},{9,10},{10,11},{12,13},{... | collective-permute-start | bytes 208904 | tf_op jit(solution)/shard_map/ppermute | solution.py:220
  21.2 1.9 %collective-permute-start.3 = (bf16[16,2176]{1,0:T(8,128)(2,1)S(1)}, bf16[16,2176]{1,0:T(8,128)(2,1)S(1)}, u32[]{:S(2)}, u32[]{:S(2)}) collective-permute-start(bf16[16,2176]{1,0:T(8,128)(2,1)S(1)} %get-tuple-element.15), channel_id=1, source_target_pairs={{1,0},{2,1},{3,2},{5,4},{6,5},{7,6},{9,8},{10,9},{11,10},{13,12},{... | collective-permute-start | bytes 208904 | tf_op jit(solution)/shard_map/ppermute | solution.py:220
  23.2 3.7 %collective-permute-done.3 = bf16[16,2176]{1,0:T(8,128)(2,1)S(1)} collective-permute-done((bf16[16,2176]{1,0:T(8,128)(2,1)S(1)}, bf16[16,2176]{1,0:T(8,128)(2,1)S(1)}, u32[]{:S(2)}, u32[]{:S(2)}) %collective-permute-start.3) | collective-permute-done | bytes 69664 | tf_op jit(solution)/shard_map/ppermute | solution.py:220
  27.1 1.2 %constant_dynamic-slice_fusion.1 = (bf16[288,2176]{1,0:T(8,128)(2,1)S(1)}, bf16[288,2176]{1,0:T(8,128)(2,1)}) fusion(bf16[544,2176]{1,0:T(8,128)(2,1)S(1)} %pad_maximum_fusion, s32[]{:T(128)S(6)} %select_n.55, s32[]{:T(128)S(6)} %select_n.54), kind=kLoop, calls=%fused_computation.72 | loop fusion | bytes 5013512 | tf_op jit(solution)/shard_map/dynamic_slice | solution.py:281
  28.3 1.2 %collective-permute-start.4 = (bf16[288,2176]{1,0:T(8,128)(2,1)S(1)}, bf16[288,2176]{1,0:T(8,128)(2,1)S(1)}, u32[]{:S(2)}, u32[]{:S(2)}) collective-permute-start(bf16[288,2176]{1,0:T(8,128)(2,1)S(1)} %get-tuple-element.12), channel_id=1, source_target_pairs={{0,16},{16,0},{1,17},{17,1},{2,18},{18,2},{3,19},{19,3},{4,20},{20... | collective-permute-start | bytes 3760136 | tf_op jit(solution)/shard_map/ppermute | solution.py:280
  29.9 26.2 %collective-permute-done.5 = f32[3,16,64]{2,1,0:T(8,128)S(1)} collective-permute-done((f32[3,16,64]{2,1,0:T(8,128)S(1)}, f32[3,16,64]{2,1,0:T(8,128)S(1)}, u32[]{:S(2)}, u32[]{:S(2)}) %collective-permute-start.5) | collective-permute-done | bytes 12320 | tf_op jit(solution)/shard_map/ppermute | solution.py:285
  56.3 0.9 reshape.65.offsets_ref
  57.2 1.0 copy-done
  58.3 30.3 %shard_map.113 = f32[16,8,128]{2,1,0:T(8,128)} custom-call(f32[1]{0:T(128)} %bitcast.sign_ref, bf16[288,2176]{1,0:T(8,128)(2,1)} %get-tuple-element.13.mine_ref, bf16[288,2176]{1,0:T(8,128)(2,1)} %copy-done, f32[2,8,4096]{2,1,0:T(8,128)} %reshape.65.offsets_ref, bf16[80,64]{1,0:T(8,128)(2,1)} %constant.44.clone.row_ref, ...), custom_call_target="tpu_custom_call" | custom-call | tf_op jit(solution)/shard_map/pallas_call | solution.py:193
  88.5 1.0 copy.92
  90.0 1.3 %collective-permute-start.6 = (f32[3,8,64]{2,1,0:T(8,128)S(1)}, f32[3,8,64]{2,1,0:T(8,128)S(1)}, u32[]{:S(2)}, u32[]{:S(2)}) collective-permute-start(f32[3,8,64]{2,1,0:T(8,128)S(1)} %pad_maximum_fusion.7), channel_id=1, source_target_pairs={{0,16},{16,0},{1,17},{17,1},{2,18},{18,2},{3,19},{19,3},{4,20},{20... | collective-permute-start | bytes 18440 | tf_op jit(solution)/shard_map/ppermute | solution.py:292
  91.2 1.3 %collective-permute-done.6 = f32[3,8,64]{2,1,0:T(8,128)S(1)} collective-permute-done((f32[3,8,64]{2,1,0:T(8,128)S(1)}, f32[3,8,64]{2,1,0:T(8,128)S(1)}, u32[]{:S(2)}, u32[]{:S(2)}) %collective-permute-start.6) | collective-permute-done | bytes 6176 | tf_op jit(solution)/shard_map/ppermute | solution.py:292
  92.8 3.2 %collective-permute-start.7 = (f32[4,2,16,3]{3,2,1,0:T(8,128)S(1)}, f32[4,2,16,3]{3,2,1,0:T(8,128)S(1)}, u32[]{:S(2)}, u32[]{:S(2)}) collective-permute-start(f32[4,2,16,3]{3,2,1,0:T(8,128)S(1)} %get-tuple-element.24), channel_id=1, source_target_pairs={{0,4},{4,8},{8,12},{1,5},{5,9},{9,13},{2,6},{6,10},{10,14},{3,7},{... | collective-permute-start | bytes 4616 | tf_op jit(solution)/shard_map/ppermute | solution.py:220
  96.0 1.3 %collective-permute-start.8 = (f32[4,2,16,3]{3,2,1,0:T(8,128)S(1)}, f32[4,2,16,3]{3,2,1,0:T(8,128)S(1)}, u32[]{:S(2)}, u32[]{:S(2)}) collective-permute-start(f32[4,2,16,3]{3,2,1,0:T(8,128)S(1)} %get-tuple-element.25), channel_id=1, source_target_pairs={{4,0},{8,4},{12,8},{5,1},{9,5},{13,9},{6,2},{10,6},{14,10},{7,3},{... | collective-permute-start | bytes 4616 | tf_op jit(solution)/shard_map/ppermute | solution.py:220
  97.7 3.9 %collective-permute-done.8 = f32[4,2,16,3]{3,2,1,0:T(8,128)S(1)} collective-permute-done((f32[4,2,16,3]{3,2,1,0:T(8,128)S(1)}, f32[4,2,16,3]{3,2,1,0:T(8,128)S(1)}, u32[]{:S(2)}, u32[]{:S(2)}) %collective-permute-start.8) | collective-permute-done | bytes 1568 | tf_op jit(solution)/shard_map/ppermute | solution.py:220
  101.7 3.8 %collective-permute-start.9 = (f32[4,2,3,70]{3,1,2,0:T(2,128)S(1)}, f32[4,2,3,70]{3,1,2,0:T(2,128)S(1)}, u32[]{:S(2)}, u32[]{:S(2)}) collective-permute-start(f32[4,2,3,70]{3,1,2,0:T(2,128)S(1)} %copy.106), channel_id=1, source_target_pairs={{0,1},{1,2},{2,3},{4,5},{5,6},{6,7},{8,9},{9,10},{10,11},{12,13},{... | collective-permute-start | bytes 20168 | tf_op jit(solution)/shard_map/ppermute | solution.py:220
  105.5 1.9 %collective-permute-start.10 = (f32[4,2,3,70]{3,1,2,0:T(2,128)S(1)}, f32[4,2,3,70]{3,1,2,0:T(2,128)S(1)}, u32[]{:S(2)}, u32[]{:S(2)}) collective-permute-start(f32[4,2,3,70]{3,1,2,0:T(2,128)S(1)} %copy.107), channel_id=1, source_target_pairs={{1,0},{2,1},{3,2},{5,4},{6,5},{7,6},{9,8},{10,9},{11,10},{13,12},{... | collective-permute-start | bytes 20168 | tf_op jit(solution)/shard_map/ppermute | solution.py:220
  107.5 3.0 %collective-permute-done.10 = f32[4,2,3,70]{3,1,2,0:T(2,128)S(1)} collective-permute-done((f32[4,2,3,70]{3,1,2,0:T(2,128)S(1)}, f32[4,2,3,70]{3,1,2,0:T(2,128)S(1)}, u32[]{:S(2)}, u32[]{:S(2)}) %collective-permute-start.10) | collective-permute-done | bytes 6752 | tf_op jit(solution)/shard_map/ppermute | solution.py:220
  (55 shorter events, 3.9 us)
Async XLA Ops:
  1.7 6.2 %collective-permute-start = (bf16[512,16]{1,0:T(8,128)(2,1)S(1)}, bf16[512,16]{1,0:T(8,128)(2,1)S(1)}, u32[]{:S(2)}, u32[]{:S(2)}) collective-permute-start(bf16[512,16]{1,0:T(8,128)(2,1)S(1)} %get-tuple-element.17), channel_id=1, source_target_pairs={{0,4},{4,8},{8,12},{1,5},{5,9},{9,13},{2,6},{6,10},{10,14},{3,7},{... | collective-permute-start | bytes 49160 | tf_op jit(solution)/shard_map/ppermute | solution.py:220
  5.8 5.7 %collective-permute-start.1 = (bf16[512,16]{1,0:T(8,128)(2,1)S(1)}, bf16[512,16]{1,0:T(8,128)(2,1)S(1)}, u32[]{:S(2)}, u32[]{:S(2)}) collective-permute-start(bf16[512,16]{1,0:T(8,128)(2,1)S(1)} %get-tuple-element.16), channel_id=1, source_target_pairs={{4,0},{8,4},{12,8},{5,1},{9,5},{13,9},{6,2},{10,6},{14,10},{7,3},{... | collective-permute-start | bytes 49160 | tf_op jit(solution)/shard_map/ppermute | solution.py:220
  16.1 7.1 %collective-permute-start.2 = (bf16[16,2176]{1,0:T(8,128)(2,1)S(1)}, bf16[16,2176]{1,0:T(8,128)(2,1)S(1)}, u32[]{:S(2)}, u32[]{:S(2)}) collective-permute-start(bf16[16,2176]{1,0:T(8,128)(2,1)S(1)} %get-tuple-element.14), channel_id=1, source_target_pairs={{0,1},{1,2},{2,3},{4,5},{5,6},{6,7},{8,9},{9,10},{10,11},{12,13},{... | collective-permute-start | bytes 208904 | tf_op jit(solution)/shard_map/ppermute | solution.py:220
  21.2 5.6 %collective-permute-start.3 = (bf16[16,2176]{1,0:T(8,128)(2,1)S(1)}, bf16[16,2176]{1,0:T(8,128)(2,1)S(1)}, u32[]{:S(2)}, u32[]{:S(2)}) collective-permute-start(bf16[16,2176]{1,0:T(8,128)(2,1)S(1)} %get-tuple-element.15), channel_id=1, source_target_pairs={{1,0},{2,1},{3,2},{5,4},{6,5},{7,6},{9,8},{10,9},{11,10},{13,12},{... | collective-permute-start | bytes 208904 | tf_op jit(solution)/shard_map/ppermute | solution.py:220
  27.1 2.5 %copy-start.2 = (s32[1,16,64]{2,1,0:T(8,128)S(1)}, s32[1,16,64]{2,1,0:T(8,128)}, u32[]{:S(2)}) copy-start(s32[1,16,64]{2,1,0:T(8,128)} %param.11) | copy-start | bytes 12292
  27.1 2.5 %copy-start.1 = (s32[2,1,16,64]{3,2,1,0:T(8,128)S(1)}, s32[2,1,16,64]{3,2,1,0:T(8,128)}, u32[]{:S(2)}) copy-start(s32[2,1,16,64]{3,2,1,0:T(8,128)} %param.12) | copy-start | bytes 24580
  28.3 28.9 %collective-permute-start.4 = (bf16[288,2176]{1,0:T(8,128)(2,1)S(1)}, bf16[288,2176]{1,0:T(8,128)(2,1)S(1)}, u32[]{:S(2)}, u32[]{:S(2)}) collective-permute-start(bf16[288,2176]{1,0:T(8,128)(2,1)S(1)} %get-tuple-element.12), channel_id=1, source_target_pairs={{0,16},{16,0},{1,17},{17,1},{2,18},{18,2},{3,19},{19,3},{4,20},{20... | collective-permute-start | bytes 3760136 | tf_op jit(solution)/shard_map/ppermute | solution.py:280
  29.5 26.6 %collective-permute-start.5 = (f32[3,16,64]{2,1,0:T(8,128)S(1)}, f32[3,16,64]{2,1,0:T(8,128)S(1)}, u32[]{:S(2)}, u32[]{:S(2)}) collective-permute-start(f32[3,16,64]{2,1,0:T(8,128)S(1)} %pad_maximum_fusion.4), channel_id=1, source_target_pairs={{0,16},{16,0},{1,17},{17,1},{2,18},{18,2},{3,19},{19,3},{4,20},{20... | collective-permute-start | bytes 36872 | tf_op jit(solution)/shard_map/ppermute | solution.py:285
  57.2 1.0 copy-start
  90.0 2.6 %collective-permute-start.6 = (f32[3,8,64]{2,1,0:T(8,128)S(1)}, f32[3,8,64]{2,1,0:T(8,128)S(1)}, u32[]{:S(2)}, u32[]{:S(2)}) collective-permute-start(f32[3,8,64]{2,1,0:T(8,128)S(1)} %pad_maximum_fusion.7), channel_id=1, source_target_pairs={{0,16},{16,0},{1,17},{17,1},{2,18},{18,2},{3,19},{19,3},{4,20},{20... | collective-permute-start | bytes 18440 | tf_op jit(solution)/shard_map/ppermute | solution.py:292
  92.8 4.9 %collective-permute-start.7 = (f32[4,2,16,3]{3,2,1,0:T(8,128)S(1)}, f32[4,2,16,3]{3,2,1,0:T(8,128)S(1)}, u32[]{:S(2)}, u32[]{:S(2)}) collective-permute-start(f32[4,2,16,3]{3,2,1,0:T(8,128)S(1)} %get-tuple-element.24), channel_id=1, source_target_pairs={{0,4},{4,8},{8,12},{1,5},{5,9},{9,13},{2,6},{6,10},{10,14},{3,7},{... | collective-permute-start | bytes 4616 | tf_op jit(solution)/shard_map/ppermute | solution.py:220
  96.0 5.6 %collective-permute-start.8 = (f32[4,2,16,3]{3,2,1,0:T(8,128)S(1)}, f32[4,2,16,3]{3,2,1,0:T(8,128)S(1)}, u32[]{:S(2)}, u32[]{:S(2)}) collective-permute-start(f32[4,2,16,3]{3,2,1,0:T(8,128)S(1)} %get-tuple-element.25), channel_id=1, source_target_pairs={{4,0},{8,4},{12,8},{5,1},{9,5},{13,9},{6,2},{10,6},{14,10},{7,3},{... | collective-permute-start | bytes 4616 | tf_op jit(solution)/shard_map/ppermute | solution.py:220
  101.7 5.8 %collective-permute-start.9 = (f32[4,2,3,70]{3,1,2,0:T(2,128)S(1)}, f32[4,2,3,70]{3,1,2,0:T(2,128)S(1)}, u32[]{:S(2)}, u32[]{:S(2)}) collective-permute-start(f32[4,2,3,70]{3,1,2,0:T(2,128)S(1)} %copy.106), channel_id=1, source_target_pairs={{0,1},{1,2},{2,3},{4,5},{5,6},{6,7},{8,9},{9,10},{10,11},{12,13},{... | collective-permute-start | bytes 20168 | tf_op jit(solution)/shard_map/ppermute | solution.py:220
  105.5 5.0 %collective-permute-start.10 = (f32[4,2,3,70]{3,1,2,0:T(2,128)S(1)}, f32[4,2,3,70]{3,1,2,0:T(2,128)S(1)}, u32[]{:S(2)}, u32[]{:S(2)}) collective-permute-start(f32[4,2,3,70]{3,1,2,0:T(2,128)S(1)} %copy.107), channel_id=1, source_target_pairs={{1,0},{2,1},{3,2},{5,4},{6,5},{7,6},{9,8},{10,9},{11,10},{13,12},{... | collective-permute-start | bytes 20168 | tf_op jit(solution)/shard_map/ppermute | solution.py:220

commit v2 on v1

v2 whole, which is shorter than its diff:
```python
import functools
import math

import jax
import jax.numpy as jnp
import ml_dtypes
import numpy as np
from jax import lax
from jax.experimental import pallas as pl
from jax.experimental.pallas import tpu as pltpu
from jax.sharding import PartitionSpec as P

PATCH = 64
REACH = 12
SPACING = 32
ITERS = 3
BOUND = 8
FAR = BOUND + REACH
LAG_ROWS = 48
HALF = PATCH // 2
MARGIN = SPACING // 2
LANES = 128
BLOCK = 256
MESH = pl.DeviceIdType.MESH

sharpness = 32.0
tiny_energy = 1e-06


def bf16(table):
    return np.asarray(table, np.float32).astype(ml_dtypes.bfloat16)


def split(table):
    high = bf16(table)
    return high, bf16(np.asarray(table, np.float32) - high.astype(np.float32))


@functools.lru_cache(None)
def tables():
    n = np.arange(PATCH)
    angle = 2.0 * math.pi * ((n[:, None] * n[None, :]) % PATCH) / PATCH
    cosine, sine = np.cos(angle), np.sin(angle)
    row_table = np.zeros((80, PATCH))
    row_table[:HALF] = cosine[:HALF]
    row_table[HALF:PATCH] = -sine[:HALF]
    row_table[PATCH] = cosine[HALF]
    second = np.zeros((2, 256, 2, 2, 2, PATCH))
    spread = np.zeros((256, 4, PATCH))
    for pair in range(2):
        for q in range(2):
            node = 2 * pair + q
            rows = slice(MARGIN + SPACING * node, MARGIN + SPACING * node + PATCH)
            second[0, rows, pair, 0, q] = cosine.T
            second[0, rows, pair, 1, q] = -sine.T
            second[1, rows, pair, 0, q] = sine.T
            second[1, rows, pair, 1, q] = cosine.T
            spread[rows, node] = 1.0
    lags = np.arange(2 * FAR + 1) - FAR
    lag_angle = 2.0 * math.pi * ((n[:, None] * lags[None, :]) % PATCH) / PATCH
    lag_cos, lag_sin = np.cos(lag_angle), np.sin(lag_angle)
    back = np.zeros((2, 2, PATCH, 2, 2, PATCH))
    for q in range(2):
        back[0, q, :, 0, q, : lags.size] = lag_cos
        back[1, q, :, 0, q, : lags.size] = -lag_sin
        back[0, q, :, 1, q, : lags.size] = lag_sin
        back[1, q, :, 1, q, : lags.size] = lag_cos
    back_high, back_low = split(back.reshape(256, 256))
    fold = np.where(np.arange(HALF) == 0, 1.0, 2.0)[None]
    rows = np.zeros((LAG_ROWS, 2 * HALF))
    rows[: lags.size, :HALF] = fold * lag_cos[:HALF].T
    rows[: lags.size, HALF:] = -fold * lag_sin[:HALF].T
    row_high, row_low = split(rows)
    row_back = np.concatenate([row_high, row_high, row_low], 1)
    gather = np.zeros((2, 4, PATCH, 128))
    lane_lag = np.arange(PATCH) - FAR
    for node in range(4):
        gather[0, node, :, node] = 1.0
        gather[0, node, :, 4 + node] = lane_lag
        gather[1, node, :, 8 + node] = 1.0
    return (
        bf16(row_table),
        bf16(second.reshape(2, 256, 512)),
        np.asarray(spread.reshape(256, 256), np.float32),
        back_high,
        back_low,
        row_back,
        np.asarray(gather.reshape(2, 256, 128), np.float32),
    )


def match_core(
    node_rows,
    strips_ref,
    offsets_ref,
    row_ref,
    second_ref,
    spread_ref,
    back_high_ref,
    back_low_ref,
    row_back_ref,
    gather_ref,
    out_ref,
    half_ref,
    nyquist_ref,
    squares_ref,
    arrive,
):
    f32, b16 = jnp.float32, jnp.bfloat16
    blocks = strips_ref.shape[2] // BLOCK

    def dot(a, b):
        return jnp.dot(a, b, preferred_element_type=f32)

    def exact(a, b):
        return jnp.dot(a, b, preferred_element_type=f32, precision=lax.Precision.HIGHEST)

    def over_rows(block):
        lanes = pl.ds(pl.multiple_of(block * BLOCK, BLOCK), BLOCK)
        for which in range(2):
            for i in range(node_rows):
                rows = strips_ref[which, i * SPACING : i * SPACING + PATCH, lanes]
                got = dot(row_ref[...], rows)
                half_ref[which, 0, i * HALF : (i + 1) * HALF, lanes] = got[:HALF].astype(b16)
                half_ref[which, 1, i * HALF : (i + 1) * HALF, lanes] = got[HALF:PATCH].astype(b16)
                nyquist_ref[which, i : i + 1, lanes] = (
                    got[PATCH : PATCH + 1].astype(b16).astype(f32)
                )
                wide = rows.astype(f32)
                squares_ref[which, i : i + 1, lanes] = jnp.sum(wide * wide, axis=0, keepdims=True)

    row_lag = lax.broadcasted_iota(jnp.int32, (LAG_ROWS, BLOCK), 0) - FAR
    col_lag = (lax.broadcasted_iota(jnp.int32, (LAG_ROWS, BLOCK), 1) & (PATCH - 1)) - FAR
    alternate = jnp.where((row_lag & 1) == 0, 1.0, -1.0).astype(f32)
    row_lag = row_lag.astype(f32)
    col_lag = col_lag.astype(f32)

    def over_columns(first, then, pair):
        real, imag = slice(256 * pair, 256 * pair + 128), slice(256 * pair + 128, 256 * pair + 256)
        cross_real = first[:, real] * then[:, real] + first[:, imag] * then[:, imag]
        cross_imag = first[:, real] * then[:, imag] - first[:, imag] * then[:, real]
        cross = jnp.concatenate([cross_real, cross_imag], 1)
        high = cross.astype(b16)
        low = (cross - high.astype(f32)).astype(b16)
        return dot(high, back_high_ref[...]) + dot(low, back_high_ref[...]) + dot(high, back_low_ref[...])

    def four_columns(group):
        lanes = pl.ds(pl.multiple_of((group + 1) * LANES, LANES), BLOCK)
        spectra, edges, energies = [], [], []
        for which in range(2):
            spectra.append(
                dot(half_ref[which, 0, :, lanes], second_ref[0])
                + dot(half_ref[which, 1, :, lanes], second_ref[1])
            )
            edges.append(dot(nyquist_ref[which, :, lanes].astype(b16), second_ref[0]))
            energies.append(exact(squares_ref[which, :, lanes], spread_ref[...]))
        scale = (sharpness / (PATCH * PATCH)) / jnp.sqrt(energies[0] * energies[1] + tiny_energy)
        columns = [over_columns(spectra[0], spectra[1], pair) for pair in range(2)]
        edge_columns = jnp.concatenate(
            [over_columns(edges[0], edges[1], pair)[:, :128] for pair in range(2)], 1
        )
        here = pl.ds(pl.multiple_of(group * BLOCK, BLOCK), BLOCK)
        row_offset = offsets_ref[0, :, here]
        col_offset = offsets_ref[1, :, here]
        totals, row_totals = [], []
        for i in range(node_rows):
            rows = slice(i * HALF, (i + 1) * HALF)
            field = jnp.concatenate(
                [
                    jnp.concatenate([columns[0][rows, :128], columns[1][rows, :128]], 1),
                    jnp.concatenate([columns[0][rows, 128:], columns[1][rows, 128:]], 1),
                ],
                0,
            )
            high = field.astype(b16)
            low = (field - high.astype(f32)).astype(b16)
            found = dot(row_back_ref[...], jnp.concatenate([high, low, high], 0))
            found = found + alternate * edge_columns[i : i + 1]
            inside = (jnp.abs(row_lag - row_offset[i : i + 1]) <= REACH) & (
                jnp.abs(col_lag - col_offset[i : i + 1]) <= REACH
            )
            weights = jnp.where(inside, jnp.exp(found * scale[i : i + 1]), 0.0)
            totals.append(jnp.sum(weights, axis=0, keepdims=True))
            row_totals.append(jnp.sum(weights * row_lag, axis=0, keepdims=True))
        out_ref[group] = exact(jnp.concatenate(totals, 0), gather_ref[0]) + exact(
            jnp.concatenate(row_totals, 0), gather_ref[1]
        )

    over_rows(0)

    def one(block, _):
        arrive(block)
        over_rows(block + 1)
        four_columns(2 * block)
        four_columns(2 * block + 1)
        return 0

    lax.fori_loop(0, blocks - 2, one, 0)
    over_rows(blocks - 1)
    four_columns(2 * (blocks - 2))


def plain_kernel(node_rows, *refs):
    match_core(node_rows, *refs, lambda block: None)


def pair_kernel(counts, node_rows, own_ref, *refs):
    (strips_ref, local_sem, send_sem, recv_sem, main_send, main_recv) = refs[-6:]
    slabs, columns, rows_of = counts
    z, x, y = lax.axis_index("gz"), lax.axis_index("gx"), lax.axis_index("gy")
    height, width = own_ref.shape
    main = node_rows * SPACING + MARGIN
    strip = main + MARGIN
    zero = jnp.bfloat16(0)
    strips_ref[:, :MARGIN, :] = jnp.full((2, MARGIN, width + 2 * BLOCK), zero)
    strips_ref[:, main:, :] = jnp.full((2, MARGIN, width + 2 * BLOCK), zero)
    strips_ref[:, :, :BLOCK] = jnp.full((2, strip, BLOCK), zero)
    strips_ref[:, :, BLOCK + width :] = jnp.full((2, strip, BLOCK), zero)

    def rows_at(start, size):
        return pl.ds(pl.multiple_of(start, MARGIN), size)

    def source_main(slab):
        return rows_at(slab * (height - main), main)

    def landed_main(slab):
        return rows_at((1 - slab) * MARGIN, main)

    def source_edge(slab):
        return rows_at((1 - slab) * (height - MARGIN), MARGIN)

    def landed_edge(slab):
        return rows_at(slab * main, MARGIN)

    left, right, centre = pl.ds(BLOCK - LANES, LANES), pl.ds(BLOCK + width, LANES), pl.ds(BLOCK, width)
    sides = (
        (1, pl.ds(width - LANES, LANES), left),
        (-1, pl.ds(0, LANES), right),
        (0, pl.ds(0, width), centre),
    )

    def inside(place, count):
        return (place >= 0) & (place < count)

    pieces = []
    for other in range(2):
        slab = z if other == 0 else 1 - z
        for vertical in range(2):
            for number, (shift, source_lanes, landed_lanes) in enumerate(sides):
                if shift == 0 and vertical == 0:
                    continue
                slot = (other * 2 + vertical) * 3 + number
                down = (1 - 2 * slab) * vertical
                source = (source_edge if vertical else source_main)(slab)
                landed = (landed_edge if vertical else landed_main)(slab)
                sent = pltpu.make_async_remote_copy(
                    src_ref=own_ref.at[source, source_lanes],
                    dst_ref=strips_ref.at[z, landed, landed_lanes],
                    send_sem=send_sem.at[slot],
                    recv_sem=recv_sem.at[slot],
                    device_id=(slab, x + shift, y + down),
                    device_id_type=MESH,
                )
                is_sent = inside(x + shift, columns) & inside(y + down, rows_of)
                mine = (landed_edge if vertical else landed_main)(z)
                up = (1 - 2 * z) * vertical
                giver = (slab, x - shift, y - up)
                comes = pltpu.make_async_remote_copy(
                    src_ref=own_ref.at[source, source_lanes],
                    dst_ref=strips_ref.at[slab, mine, landed_lanes],
                    send_sem=send_sem.at[slot],
                    recv_sem=recv_sem.at[slot],
                    device_id=giver,
                    device_id_type=MESH,
                )
                does_come = inside(x - shift, columns) & inside(y - up, rows_of)
                pieces.append((sent, is_sent, comes, does_come, giver))

    barrier = pltpu.get_barrier_semaphore()
    pl.semaphore_signal(barrier, inc=1, device_id=(1 - z, x, y), device_id_type=MESH)
    targets = jnp.int32(1)
    for _, is_sent, _, does_come, giver in pieces:

        @pl.when(does_come)
        def _():
            pl.semaphore_signal(barrier, inc=1, device_id=giver, device_id_type=MESH)

        targets = targets + is_sent.astype(jnp.int32)
    local = pltpu.make_async_copy(
        own_ref.at[source_main(z)], strips_ref.at[z, landed_main(z), centre], local_sem
    )
    local.start()
    pl.semaphore_wait(barrier, targets)

    for sent, is_sent, _, _, _ in pieces:
        pl.when(is_sent)(sent.start)

    def block_copy(block, section, slab):
        at = pl.multiple_of(block * BLOCK, BLOCK)
        return pltpu.make_async_remote_copy(
            src_ref=own_ref.at[source_main(1 - z), pl.ds(at, BLOCK)],
            dst_ref=strips_ref.at[section, landed_main(slab), pl.ds(BLOCK + at, BLOCK)],
            send_sem=main_send.at[block],
            recv_sem=main_recv.at[block],
            device_id=(1 - z, x, y),
            device_id_type=MESH,
        )

    blocks = width // BLOCK

    def start(block, _):
        block_copy(block, z, 1 - z).start()
        return 0

    lax.fori_loop(0, blocks, start, 0)
    local.wait()
    for _, _, comes, does_come, _ in pieces:
        pl.when(does_come)(comes.wait_recv)

    match_core(node_rows, strips_ref, *refs[:-6], lambda block: block_copy(block, 1 - z, z).wait_recv())

    def finish(block, _):
        block_copy(block, z, 1 - z).wait_send()
        return 0

    lax.fori_loop(0, blocks, finish, 0)
    for sent, is_sent, _, _, _ in pieces:
        pl.when(is_sent)(sent.wait_send)


def match(pixels, offsets, counts=None):
    node_rows, node_cols = offsets.shape[1:]
    groups = node_cols // 4 + 1
    width = node_cols * SPACING + 2 * BLOCK
    constants = [jnp.asarray(table) for table in tables()]
    shifted = jnp.pad(offsets.astype(jnp.float32), ((0, 0), (0, 0), (3, 1)))
    spread_offsets = jnp.repeat(shifted, PATCH, axis=2)
    scratch = [
        pltpu.VMEM((2, 2, node_rows * HALF, width), jnp.bfloat16),
        pltpu.VMEM((2, node_rows, width), jnp.float32),
        pltpu.VMEM((2, node_rows, width), jnp.float32),
    ]
    vmem = pl.BlockSpec(memory_space=pltpu.VMEM)
    specs = [vmem] * (2 + len(constants))
    if counts is None:
        body = functools.partial(plain_kernel, node_rows)
        params = pltpu.CompilerParams(vmem_limit_bytes=56 * 1024 * 1024)
    else:
        body = functools.partial(pair_kernel, counts, node_rows)
        params = pltpu.CompilerParams(
            vmem_limit_bytes=56 * 1024 * 1024, collective_id=0, has_side_effects=True
        )
        specs[0] = pl.BlockSpec(memory_space=pl.ANY)
        blocks = width // BLOCK - 2
        scratch += [
            pltpu.VMEM((2, (node_rows + 1) * SPACING, width), jnp.bfloat16),
            pltpu.SemaphoreType.DMA,
            pltpu.SemaphoreType.DMA((12,)),
            pltpu.SemaphoreType.DMA((12,)),
            pltpu.SemaphoreType.DMA((blocks,)),
            pltpu.SemaphoreType.DMA((blocks,)),
        ]
    out = pl.pallas_call(
        body,
        out_shape=jax.ShapeDtypeStruct((groups, node_rows, 128), jnp.float32),
        in_specs=specs,
        out_specs=vmem,
        scratch_shapes=scratch,
        compiler_params=params,
    )(pixels, spread_offsets, *constants)
    sums = jnp.transpose(out[:, :, :12].reshape(groups, node_rows, 3, 4), (2, 1, 0, 3))
    sums = sums.reshape(3, node_rows, 4 * groups)[:, :, 3:-1]
    return jnp.stack([sums[2] / sums[0], sums[1] / sums[0], sums[0]], 0)


def beside(value, axis, steps):
    count = lax.axis_size(axis)
    pairs = [(i, i + steps) for i in range(count) if 0 <= i + steps < count]
    return lax.ppermute(value, axis, pairs)


def bordered(field, axis, dim, width):
    length = field.shape[dim]
    before = beside(lax.slice_in_dim(field, length - width, length, axis=dim), axis, 1)
    after = beside(lax.slice_in_dim(field, 0, width, axis=dim), axis, -1)
    return before, after


def neighbour_sum(padded):
    return (
        padded[..., :-2, 1:-1]
        + padded[..., 2:, 1:-1]
        + padded[..., 1:-1, :-2]
        + padded[..., 1:-1, 2:]
    )


def relax(target, stiffness, living):
    fields = jnp.concatenate([target, stiffness[None], living[None]], 0)
    before, after = bordered(fields, "gx", 3, ITERS)
    fields = jnp.concatenate([before, fields, after], 3)
    before, after = bordered(fields, "gy", 2, ITERS)
    fields = jnp.concatenate([before, fields, after], 2)
    target, stiffness, living = fields[:2], fields[2], fields[3]
    moved = living[None] * target
    for _ in range(ITERS):
        pulled = neighbour_sum(living[None] * moved)
        count = neighbour_sum(living)
        inner = (slice(None), slice(1, -1), slice(1, -1))
        target, moved = target[(slice(None),) + inner], moved[(slice(None),) + inner]
        stiffness, living = stiffness[inner], living[inner]
        moved = (moved + stiffness[None] * target + living[None] * pulled) / (
            1.0 + stiffness + living * count
        )[None]
    return moved


def shards(section_pixels, tissue, peak_offsets):
    own = section_pixels[0]
    pixel_rows, pixel_cols = own.shape
    node_rows = pixel_rows // SPACING
    slabs = lax.axis_size("gz")
    place = lax.axis_index("gz")
    offsets = peak_offsets[:, 0].astype(jnp.float32)
    living = tissue.astype(jnp.float32)
    per_node = jnp.float32((2 * REACH + 1) ** 2)

    if slabs == 2 and node_rows % 16 == 0 and pixel_cols % BLOCK == 0:
        half_rows = node_rows // 2
        swap = [(0, 1), (1, 0)]
        first = place == 0
        nodes = jnp.concatenate([offsets, living], 0)
        other_nodes = lax.ppermute(nodes, "gz", swap)
        nodes_0 = jnp.where(first, nodes, other_nodes)
        nodes_1 = jnp.where(first, other_nodes, nodes)
        counts = tuple(lax.axis_size(axis) for axis in ("gz", "gx", "gy"))
        ours = match(
            own, lax.dynamic_slice_in_dim(nodes_0[:2], place * half_rows, half_rows, 1), counts
        )
        others = lax.ppermute(ours, "gz", swap)
        matched = jnp.concatenate(
            [jnp.where(first, ours, others), jnp.where(first, others, ours)], 1
        )
        target = jnp.stack([matched[:2], nodes_1[:2]], 1)
        alive = jnp.stack([nodes_0[2], nodes_1[2]], 0)
        stiffness = jnp.stack([nodes_0[2] * matched[2] / per_node, nodes_1[2]], 0)
        moved = relax(target, stiffness, alive)
        relaxed = jnp.where(first, moved[:, 0], moved[:, 1])
        placed = jnp.where(first, moved[:, 0], moved[:, 0] + moved[:, 1])
        return relaxed[:, None], placed[:, None]

    before, after = bordered(own, "gx", 1, LANES)
    own = jnp.concatenate([before, own, after], 1)
    before, after = bordered(own, "gy", 0, MARGIN)
    own = jnp.concatenate([before, own, after], 0)
    strips = jnp.pad(
        jnp.stack([own, beside(own, "gz", -1)], 0), ((0, 0), (0, 0), (BLOCK - LANES, BLOCK - LANES))
    )
    matched = match(strips, offsets)
    moved = relax(matched[:2, None], living * matched[2:] / per_node, living)
    placed = moved
    reach = 1
    while reach < slabs:
        placed = placed + beside(placed, "gz", reach)
        reach *= 2
    return moved, placed


def solution(mesh):
    placed = (P("gz", "gy", "gx"), P("gz", "gy", "gx"), P(None, "gz", "gy", "gx"))
    return jax.shard_map(
        shards,
        mesh=mesh,
        in_specs=placed,
        out_specs=(P(None, "gz", "gy", "gx"), P(None, "gz", "gy", "gx")),
        check_vma=False,
    )
```

time: 113 us -> 76.7 us (0.68)
  waiting for transfers between devices: 42.9 us -> 10.5 us
  Pallas kernels: 30.3 us -> 43.1 us
  starting transfers between devices: 25.4 us -> 15.6 us
  local copies, waits for them, and re-layouts: 10.6 us -> 2.73 us
  other arithmetic: 2.34 us -> 3.58 us
    ppermute x1, waiting for transfers between devices: 26.2 us -> 1.21 us  [shards(): other_nodes = lax.ppermute(nodes, 'gz', swap)]
    pallas_call x1, Pallas kernels: 30.3 us -> 43.1 us  [match(): pl.pallas_call(body, out_shape=jax.ShapeDtypeStruct((groups, node_rows, 1...]
    ppermute x8 -> x4, starting transfers between devices: 22.6 us -> 13.5 us  [beside(): return lax.ppermute(value, axis, pairs)]
    ppermute x8 -> x4, waiting for transfers between devices: 15.4 us -> 6.73 us  [beside(): return lax.ppermute(value, axis, pairs)]
    concatenate x1 -> x0, local copies, waits for them, and re-layouts: 4.58 us -> none  [shards(): own = jnp.concatenate([before, own, after, spare], 1)]
    ppermute x1, starting transfers between devices: 0.32 us -> 2.04 us  [shards(): other_nodes = lax.ppermute(nodes, 'gz', swap)]
    dynamic_slice x1 -> x0, local copies, waits for them, and re-layouts: 1.23 us -> none  [shards(): lax.dynamic_slice_in_dim(own, (1 - place) * (half_rows * SPACING), strip, 0)]
    ppermute x1, starting transfers between devices: 1.26 us -> 0.04 us  [shards(): others = lax.ppermute(ours, 'gz', swap)]
  transfers between devices with their start and end apart: 11 -> 6, of which waited for: 8 -> 4; matrix products, arithmetic and copies ran while one was open for 1% -> 0% of each run, Pallas kernels for 0% -> 0%
where the time goes in v2:
time: 76.7 us; the launch traced here: 76.3 us
  Pallas kernels  43.1 us (56%)
  starting transfers between devices  15.6 us (20%)
  waiting for transfers between devices  10.5 us (14%)
  other arithmetic  3.58 us (5%)
  local copies, waits for them, and re-layouts  2.73 us (4%)
  between operations  0.88 us (1%)
    pallas_call x1, Pallas kernels, match(): pl.pallas_call(body, out_shape=jax.ShapeDtypeStruct((groups, node_rows, 1...  43.1 us
    ppermute x4, starting transfers between devices, beside(): return lax.ppermute(value, axis, pairs)  13.5 us
    ppermute x4, waiting for transfers between devices, beside(): return lax.ppermute(value, axis, pairs)  6.73 us
    ppermute x1, waiting for transfers between devices, shards(): others = lax.ppermute(ours, 'gz', swap)  2.51 us
    ppermute x1, starting transfers between devices, shards(): other_nodes = lax.ppermute(nodes, 'gz', swap)  2.04 us
  transfers between devices with their start and end apart: 6, of which 4 were waited for; matrix products, arithmetic and copies ran while one was open for 0% of the time, Pallas kernels for 0%

profile of v2, /device:TPU:1, one launch (start us, length us, event | category | flops | bytes accessed | tf_op | source)
XLA Modules:
  0.0 76.3 jit_solution(1942284473298679903)
XLA Ops:
  0.6 0.7 convert_element_type.13
  1.3 0.7 fusion.20
  2.1 2.0 %collective-permute-start = (f32[3,16,64]{2,1,0:T(8,128)S(1)}, f32[3,16,64]{2,1,0:T(8,128)S(1)}, u32[]{:S(2)}, u32[]{:S(2)}) collective-permute-start(f32[3,16,64]{2,1,0:T(8,128)S(1)} %pad_maximum_fusion.3), channel_id=1, source_target_pairs={{0,16},{16,0},{1,17},{17,1},{2,18},{18,2},{3,19},{19,3},{4,20},{20... | collective-permute-start | bytes 36872 | tf_op jit(solution)/shard_map/ppermute | solution.py:433
  4.1 1.2 %collective-permute-done = f32[3,16,64]{2,1,0:T(8,128)S(1)} collective-permute-done((f32[3,16,64]{2,1,0:T(8,128)S(1)}, f32[3,16,64]{2,1,0:T(8,128)S(1)}, u32[]{:S(2)}, u32[]{:S(2)}) %collective-permute-start) | collective-permute-done | bytes 12320 | tf_op jit(solution)/shard_map/ppermute | solution.py:433
  5.4 0.2 broadcast_in_dim.6
  5.6 0.9 %reshape.23.refs_0_ = f32[2,8,4352]{2,1,0:T(8,128)} reshape(f32[2,8,68,64]{3,2,1,0:T(8,128)S(1)} %broadcast_in_dim.6) | data formatting | bytes 557056 | tf_op jit(solution)/shard_map/reshape | solution.py:337
  6.5 43.1 %shard_map.113 = f32[17,8,128]{2,1,0:T(8,128)} custom-call(bf16[512,2048]{1,0:T(8,128)(2,1)} %bitcast.25, f32[2,8,4352]{2,1,0:T(8,128)} %reshape.23.refs_0_, bf16[80,64]{1,0:T(8,128)(2,1)} %constant.35.clone.refs_1_, bf16[2,256,512]{2,1,0:T(8,128)(2,1)} %constant.36.clone.refs_2_, f32[256,256]{1,0:T(8,128)} %constant.37.clone.refs_3_, ...), custom_call_target="tpu_custom_call" | custom-call | tf_op jit(solution)/shard_map/pallas_call | solution.py:363
  49.6 1.0 %copy.82 = f32[17,8,12]{0,1,2:T(8,128)S(1)} copy(f32[17,8,12]{2,1,0:T(8,128)} %bitcast.26) | data formatting | bytes 13056 | tf_op jit(solution)/shard_map/slice | solution.py:371
  50.6 0.1 copy.83
  51.1 2.5 %collective-permute-done.1 = f32[3,8,64]{2,1,0:T(8,128)S(1)} collective-permute-done((f32[3,8,64]{2,1,0:T(8,128)S(1)}, f32[3,8,64]{2,1,0:T(8,128)S(1)}, u32[]{:S(2)}, u32[]{:S(2)}) %collective-permute-start.1) | collective-permute-done | bytes 6176 | tf_op jit(solution)/shard_map/ppermute | solution.py:440
  53.8 4.8 %collective-permute-start.2 = (f32[4,2,16,3]{3,2,1,0:T(8,128)S(1)}, f32[4,2,16,3]{3,2,1,0:T(8,128)S(1)}, u32[]{:S(2)}, u32[]{:S(2)}) collective-permute-start(f32[4,2,16,3]{3,2,1,0:T(8,128)S(1)} %get-tuple-element.21), channel_id=1, source_target_pairs={{0,4},{4,8},{8,12},{1,5},{5,9},{9,13},{2,6},{6,10},{10,14},{3,7},{... | collective-permute-start | bytes 4616 | tf_op jit(solution)/shard_map/ppermute | solution.py:379
  58.6 1.3 %collective-permute-start.3 = (f32[4,2,16,3]{3,2,1,0:T(8,128)S(1)}, f32[4,2,16,3]{3,2,1,0:T(8,128)S(1)}, u32[]{:S(2)}, u32[]{:S(2)}) collective-permute-start(f32[4,2,16,3]{3,2,1,0:T(8,128)S(1)} %get-tuple-element.22), channel_id=1, source_target_pairs={{4,0},{8,4},{12,8},{5,1},{9,5},{13,9},{6,2},{10,6},{14,10},{7,3},{... | collective-permute-start | bytes 4616 | tf_op jit(solution)/shard_map/ppermute | solution.py:379
  59.9 3.7 %collective-permute-done.3 = f32[4,2,16,3]{3,2,1,0:T(8,128)S(1)} collective-permute-done((f32[4,2,16,3]{3,2,1,0:T(8,128)S(1)}, f32[4,2,16,3]{3,2,1,0:T(8,128)S(1)}, u32[]{:S(2)}, u32[]{:S(2)}) %collective-permute-start.3) | collective-permute-done | bytes 1568 | tf_op jit(solution)/shard_map/ppermute | solution.py:379
  63.6 0.1 pad_maximum_fusion.1
  63.7 5.5 %collective-permute-start.4 = (f32[4,2,3,70]{3,1,2,0:T(2,128)S(1)}, f32[4,2,3,70]{3,1,2,0:T(2,128)S(1)}, u32[]{:S(2)}, u32[]{:S(2)}) collective-permute-start(f32[4,2,3,70]{3,1,2,0:T(2,128)S(1)} %copy.94), channel_id=1, source_target_pairs={{0,1},{1,2},{2,3},{4,5},{5,6},{6,7},{8,9},{9,10},{10,11},{12,13},{... | collective-permute-start | bytes 20168 | tf_op jit(solution)/shard_map/ppermute | solution.py:379
  69.3 1.9 %collective-permute-start.5 = (f32[4,2,3,70]{3,1,2,0:T(2,128)S(1)}, f32[4,2,3,70]{3,1,2,0:T(2,128)S(1)}, u32[]{:S(2)}, u32[]{:S(2)}) collective-permute-start(f32[4,2,3,70]{3,1,2,0:T(2,128)S(1)} %copy.95), channel_id=1, source_target_pairs={{1,0},{2,1},{3,2},{5,4},{6,5},{7,6},{9,8},{10,9},{11,10},{13,12},{... | collective-permute-start | bytes 20168 | tf_op jit(solution)/shard_map/ppermute | solution.py:379
  71.3 3.0 %collective-permute-done.5 = f32[4,2,3,70]{3,1,2,0:T(2,128)S(1)} collective-permute-done((f32[4,2,3,70]{3,1,2,0:T(2,128)S(1)}, f32[4,2,3,70]{3,1,2,0:T(2,128)S(1)}, u32[]{:S(2)}, u32[]{:S(2)}) %collective-permute-start.5) | collective-permute-done | bytes 6752 | tf_op jit(solution)/shard_map/ppermute | solution.py:379
  74.3 0.2 fusion.27
  74.5 0.2 fusion.28
  74.7 0.2 fusion.29
  74.9 0.3 broadcast_multiply_fusion.1
  75.2 0.3 broadcast_multiply_fusion.2
  75.5 0.2 fusion.10
  75.7 0.6 broadcast_select_fusion
  (32 shorter events, 0.7 us)
Async XLA Ops:
  2.1 3.3 %collective-permute-start = (f32[3,16,64]{2,1,0:T(8,128)S(1)}, f32[3,16,64]{2,1,0:T(8,128)S(1)}, u32[]{:S(2)}, u32[]{:S(2)}) collective-permute-start(f32[3,16,64]{2,1,0:T(8,128)S(1)} %pad_maximum_fusion.3), channel_id=1, source_target_pairs={{0,16},{16,0},{1,17},{17,1},{2,18},{18,2},{3,19},{19,3},{4,20},{20... | collective-permute-start | bytes 36872 | tf_op jit(solution)/shard_map/ppermute | solution.py:433
  51.0 2.6 %collective-permute-start.1 = (f32[3,8,64]{2,1,0:T(8,128)S(1)}, f32[3,8,64]{2,1,0:T(8,128)S(1)}, u32[]{:S(2)}, u32[]{:S(2)}) collective-permute-start(f32[3,8,64]{2,1,0:T(8,128)S(1)} %pad_maximum_fusion.6), channel_id=1, source_target_pairs={{0,16},{16,0},{1,17},{17,1},{2,18},{18,2},{3,19},{19,3},{4,20},{20... | collective-permute-start | bytes 18440 | tf_op jit(solution)/shard_map/ppermute | solution.py:440
  53.8 6.1 %collective-permute-start.2 = (f32[4,2,16,3]{3,2,1,0:T(8,128)S(1)}, f32[4,2,16,3]{3,2,1,0:T(8,128)S(1)}, u32[]{:S(2)}, u32[]{:S(2)}) collective-permute-start(f32[4,2,16,3]{3,2,1,0:T(8,128)S(1)} %get-tuple-element.21), channel_id=1, source_target_pairs={{0,4},{4,8},{8,12},{1,5},{5,9},{9,13},{2,6},{6,10},{10,14},{3,7},{... | collective-permute-start | bytes 4616 | tf_op jit(solution)/shard_map/ppermute | solution.py:379
  58.6 5.0 %collective-permute-start.3 = (f32[4,2,16,3]{3,2,1,0:T(8,128)S(1)}, f32[4,2,16,3]{3,2,1,0:T(8,128)S(1)}, u32[]{:S(2)}, u32[]{:S(2)}) collective-permute-start(f32[4,2,16,3]{3,2,1,0:T(8,128)S(1)} %get-tuple-element.22), channel_id=1, source_target_pairs={{4,0},{8,4},{12,8},{5,1},{9,5},{13,9},{6,2},{10,6},{14,10},{7,3},{... | collective-permute-start | bytes 4616 | tf_op jit(solution)/shard_map/ppermute | solution.py:379
  63.7 7.5 %collective-permute-start.4 = (f32[4,2,3,70]{3,1,2,0:T(2,128)S(1)}, f32[4,2,3,70]{3,1,2,0:T(2,128)S(1)}, u32[]{:S(2)}, u32[]{:S(2)}) collective-permute-start(f32[4,2,3,70]{3,1,2,0:T(2,128)S(1)} %copy.94), channel_id=1, source_target_pairs={{0,1},{1,2},{2,3},{4,5},{5,6},{6,7},{8,9},{9,10},{10,11},{12,13},{... | collective-permute-start | bytes 20168 | tf_op jit(solution)/shard_map/ppermute | solution.py:379
  69.3 5.0 %collective-permute-start.5 = (f32[4,2,3,70]{3,1,2,0:T(2,128)S(1)}, f32[4,2,3,70]{3,1,2,0:T(2,128)S(1)}, u32[]{:S(2)}, u32[]{:S(2)}) collective-permute-start(f32[4,2,3,70]{3,1,2,0:T(2,128)S(1)} %copy.95), channel_id=1, source_target_pairs={{1,0},{2,1},{3,2},{5,4},{6,5},{7,6},{9,8},{10,9},{11,10},{13,12},{... | collective-permute-start | bytes 20168 | tf_op jit(solution)/shard_map/ppermute | solution.py:379

commit v3 on v2

--- a/solution.py
+++ b/solution.py
@@ -92,7 +92,6 @@
 def match_core(
     node_rows,
     strips_ref,
-    offsets_ref,
     row_ref,
     second_ref,
     spread_ref,
@@ -100,11 +99,12 @@
     back_low_ref,
     row_back_ref,
     gather_ref,
-    out_ref,
     half_ref,
     nyquist_ref,
     squares_ref,
     arrive,
+    offsets_of,
+    give,
 ):
     f32, b16 = jnp.float32, jnp.bfloat16
     blocks = strips_ref.shape[2] // BLOCK
@@ -159,9 +159,7 @@
         edge_columns = jnp.concatenate(
             [over_columns(edges[0], edges[1], pair)[:, :128] for pair in range(2)], 1
         )
-        here = pl.ds(pl.multiple_of(group * BLOCK, BLOCK), BLOCK)
-        row_offset = offsets_ref[0, :, here]
-        col_offset = offsets_ref[1, :, here]
+        row_offset, col_offset = offsets_of(group)
         totals, row_totals = [], []
         for i in range(node_rows):
             rows = slice(i * HALF, (i + 1) * HALF)
@@ -182,9 +180,8 @@
             weights = jnp.where(inside, jnp.exp(found * scale[i : i + 1]), 0.0)
             totals.append(jnp.sum(weights, axis=0, keepdims=True))
             row_totals.append(jnp.sum(weights * row_lag, axis=0, keepdims=True))
-        out_ref[group] = exact(jnp.concatenate(totals, 0), gather_ref[0]) + exact(
-            jnp.concatenate(row_totals, 0), gather_ref[1]
-        )
+        sums = exact(jnp.concatenate(totals, 0), gather_ref[0])
+        give(group, sums + exact(jnp.concatenate(row_totals, 0), gather_ref[1]))
 
     over_rows(0)
 
@@ -200,12 +197,39 @@
     four_columns(2 * (blocks - 2))
 
 
-def plain_kernel(node_rows, *refs):
-    match_core(node_rows, *refs, lambda block: None)
-
-
-def pair_kernel(counts, node_rows, own_ref, *refs):
-    (strips_ref, local_sem, send_sem, recv_sem, main_send, main_recv) = refs[-6:]
+def plain_kernel(node_rows, strips_ref, offsets_ref, *refs):
+    tables_of, (out_ref, *scratch) = refs[:7], refs[7:]
+
+    def offsets_of(group):
+        here = pl.ds(pl.multiple_of(group * BLOCK, BLOCK), BLOCK)
+        return offsets_ref[0, :, here], offsets_ref[1, :, here]
+
+    def give(group, sums):
+        out_ref[group] = sums
+
+    match_core(node_rows, strips_ref, *tables_of, *scratch, lambda block: None, offsets_of, give)
+
+
+def pair_kernel(counts, node_rows, node_cols, own_ref, nodes_ref, four_ref, *refs):
+    tables_of, (out_ref, *refs) = refs[:7], refs[7:]
+    work, (
+        strips_ref,
+        sums_ref,
+        ours_ref,
+        nodes_in,
+        found_in,
+        local_sem,
+        send_sem,
+        recv_sem,
+        main_send,
+        main_recv,
+        node_sem,
+        node_send,
+        node_recv,
+        found_send,
+        found_recv,
+    ) = refs[:3], refs[3:]
+    f32 = jnp.float32
     slabs, columns, rows_of = counts
     z, x, y = lax.axis_index("gz"), lax.axis_index("gx"), lax.axis_index("gy")
     height, width = own_ref.shape
@@ -216,6 +240,9 @@
     strips_ref[:, main:, :] = jnp.full((2, MARGIN, width + 2 * BLOCK), zero)
     strips_ref[:, :, :BLOCK] = jnp.full((2, strip, BLOCK), zero)
     strips_ref[:, :, BLOCK + width :] = jnp.full((2, strip, BLOCK), zero)
+    nodes_in[...] = jnp.zeros(nodes_in.shape, f32)
+    found_in[...] = jnp.zeros(found_in.shape, f32)
+    sums_ref[...] = jnp.zeros(sums_ref.shape, f32)
 
     def rows_at(start, size):
         return pl.ds(pl.multiple_of(start, MARGIN), size)
@@ -274,25 +301,99 @@
                     device_id_type=MESH,
                 )
                 does_come = inside(x - shift, columns) & inside(y - up, rows_of)
-                pieces.append((sent, is_sent, comes, does_come, giver))
+                pieces.append((sent, is_sent, comes, does_come))
+
+    def node_source(dy):
+        if dy == 0:
+            return pl.ds(0, 2 * node_rows)
+        return pl.ds(node_rows if dy == 1 else 0, node_rows)
+
+    def node_landed(dy):
+        if dy == 0:
+            return pl.ds(node_rows, 2 * node_rows)
+        return pl.ds(0 if dy == 1 else 3 * node_rows, node_rows)
+
+    around = [
+        (other, dx, dy)
+        for other in range(2)
+        for dx in (-1, 0, 1)
+        for dy in (-1, 0, 1)
+        if (other, dx, dy) != (0, 0, 0)
+    ]
+    node_pieces = []
+    for slot, (other, dx, dy) in enumerate(around):
+        slab = z if other == 0 else 1 - z
+        copies = []
+        for section, device in ((z, (slab, x + dx, y + dy)), (slab, (slab, x - dx, y - dy))):
+            copies.append(
+                pltpu.make_async_remote_copy(
+                    src_ref=nodes_ref.at[:, node_source(dy)],
+                    dst_ref=nodes_in.at[section, 1 - dx, :, node_landed(dy)],
+                    send_sem=node_send.at[slot],
+                    recv_sem=node_recv.at[slot],
+                    device_id=device,
+                    device_id_type=MESH,
+                )
+            )
+        goes = inside(x + dx, columns) & inside(y + dy, rows_of)
+        comes = inside(x - dx, columns) & inside(y - dy, rows_of)
+        node_pieces.append((copies[0], goes, copies[1], comes))
+
+    found_pieces = []
+    for other in range(2):
+        for dx in (-1, 0, 1):
+            for vertical in range(2):
+                if (other, dx, vertical) == (0, 0, 0):
+                    continue
+                slot = (other * 3 + dx + 1) * 2 + vertical
+                slab = z if other == 0 else 1 - z
+                copies = []
+                for finder, sign in ((z, 1), (slab, -1)):
+                    down = (2 * finder - 1) * vertical
+                    row = (1 + finder) * node_rows if vertical == 0 else 3 * (1 - finder) * node_rows
+                    copies.append(
+                        (
+                            pltpu.make_async_remote_copy(
+                                src_ref=ours_ref,
+                                dst_ref=found_in.at[
+                                    1 - dx, :, pl.ds(pl.multiple_of(row, node_rows), node_rows)
+                                ],
+                                send_sem=found_send.at[slot],
+                                recv_sem=found_recv.at[slot],
+                                device_id=(slab, x + sign * dx, y + sign * down),
+                                device_id_type=MESH,
+                            ),
+                            inside(x + sign * dx, columns) & inside(y + sign * down, rows_of),
+                        )
+                    )
+                found_pieces.append(copies[0] + copies[1])
 
     barrier = pltpu.get_barrier_semaphore()
-    pl.semaphore_signal(barrier, inc=1, device_id=(1 - z, x, y), device_id_type=MESH)
-    targets = jnp.int32(1)
-    for _, is_sent, _, does_come, giver in pieces:
-
-        @pl.when(does_come)
+    targets = jnp.int32(0)
+    for other, dx, dy in around:
+        there = inside(x + dx, columns) & inside(y + dy, rows_of)
+
+        @pl.when(there)
         def _():
-            pl.semaphore_signal(barrier, inc=1, device_id=giver, device_id_type=MESH)
-
-        targets = targets + is_sent.astype(jnp.int32)
+            pl.semaphore_signal(
+                barrier,
+                inc=1,
+                device_id=(z if other == 0 else 1 - z, x + dx, y + dy),
+                device_id_type=MESH,
+            )
+
+        targets = targets + there.astype(jnp.int32)
+    own_nodes = pltpu.make_async_copy(
+        nodes_ref, nodes_in.at[z, 1, :, node_landed(0)], node_sem
+    )
+    own_nodes.start()
     local = pltpu.make_async_copy(
         own_ref.at[source_main(z)], strips_ref.at[z, landed_main(z), centre], local_sem
     )
     local.start()
     pl.semaphore_wait(barrier, targets)
 
-    for sent, is_sent, _, _, _ in pieces:
+    for sent, is_sent, _, _ in pieces + node_pieces:
         pl.when(is_sent)(sent.start)
 
     def block_copy(block, section, slab):
@@ -314,60 +415,167 @@
 
     lax.fori_loop(0, blocks, start, 0)
     local.wait()
-    for _, _, comes, does_come, _ in pieces:
+    own_nodes.wait()
+    for _, _, comes, does_come in pieces + node_pieces:
         pl.when(does_come)(comes.wait_recv)
 
-    match_core(node_rows, strips_ref, *refs[:-6], lambda block: block_copy(block, 1 - z, z).wait_recv())
+    upper = pl.ds(pl.multiple_of((1 + z) * node_rows, node_rows), node_rows)
+
+    def offsets_of(group):
+        return [
+            jnp.dot(
+                pltpu.roll(nodes_in[0, 1, part, upper, :], lax.rem(LANES - 4 * group, LANES), 1).astype(
+                    jnp.bfloat16
+                ),
+                four_ref[...],
+                preferred_element_type=f32,
+            )
+            for part in range(2)
+        ]
+
+    few = lax.broadcasted_iota(jnp.int32, (node_rows, LANES), 1)
+
+    def give(group, sums):
+        for part in range(3):
+            one = jnp.where((few >= 4 * part) & (few < 4 * part + 4), sums, 0.0)
+            sums_ref[part] += pltpu.roll(one, lax.rem(4 * group - 4 * part + LANES, LANES), 1)
+
+    match_core(
+        node_rows,
+        strips_ref,
+        *tables_of,
+        *work,
+        lambda block: block_copy(block, 1 - z, z).wait_recv(),
+        offsets_of,
+        give,
+    )
+    total = sums_ref[0]
+    held = (few >= ITERS) & (few < ITERS + node_cols)
+    ours_ref[0] = jnp.where(held, sums_ref[2] / total, 0.0)
+    ours_ref[1] = jnp.where(held, sums_ref[1] / total, 0.0)
+    ours_ref[2] = jnp.where(held, total, 0.0)
+    for sent, is_sent, _, _ in found_pieces:
+        pl.when(is_sent)(sent.start)
+    found_in[1, :, upper, :] = ours_ref[...]
+
+    lane = lax.broadcasted_iota(jnp.int32, (4 * node_rows, LANES), 1)
+
+    def joined(ref, at):
+        before = pltpu.roll(ref[at(0)], LANES - node_cols, 1)
+        after = pltpu.roll(ref[at(2)], node_cols, 1)
+        value = jnp.where(lane < ITERS, before, ref[at(1)])
+        value = jnp.where(lane < ITERS + node_cols, value, after)
+        return jnp.where(lane < 2 * ITERS + node_cols, value, 0.0)
+
+    nodes = [[joined(nodes_in, lambda k: (s, k, part)) for part in range(3)] for s in range(2)]
+    for _, _, comes, does_come in found_pieces:
+        pl.when(does_come)(comes.wait_recv)
+    found = [joined(found_in, lambda k: (k, part)) for part in range(3)]
+
+    def neighbours(value):
+        rows = 4 * node_rows
+        return (
+            pltpu.roll(value, 1, 0)
+            + pltpu.roll(value, rows - 1, 0)
+            + pltpu.roll(value, 1, 1)
+            + pltpu.roll(value, LANES - 1, 1)
+        )
+
+    per_node = float((2 * REACH + 1) ** 2)
+    moved = []
+    for section in range(2):
+        living = nodes[section][2]
+        targets = found[:2] if section == 0 else nodes[1][:2]
+        stiffness = living * found[2] / per_node if section == 0 else living
+        below = 1.0 + stiffness + living * neighbours(living)
+        for part in range(2):
+            value = living * targets[part]
+            for _ in range(ITERS):
+                value = (
+                    value + stiffness * targets[part] + living * neighbours(living * value)
+                ) / below
+            moved.append(value[node_rows : 3 * node_rows])
+    first = z == 0
+    for part in range(2):
+        out_ref[0, part] = jnp.where(first, moved[part], moved[2 + part])
+        out_ref[1, part] = jnp.where(first, moved[part], moved[part] + moved[2 + part])
 
     def finish(block, _):
         block_copy(block, z, 1 - z).wait_send()
         return 0
 
     lax.fori_loop(0, blocks, finish, 0)
-    for sent, is_sent, _, _, _ in pieces:
+    for sent, is_sent, _, _ in pieces + node_pieces + found_pieces:
         pl.when(is_sent)(sent.wait_send)
 
 
-def match(pixels, offsets, counts=None):
-    node_rows, node_cols = offsets.shape[1:]
-    groups = node_cols // 4 + 1
-    width = node_cols * SPACING + 2 * BLOCK
-    constants = [jnp.asarray(table) for table in tables()]
-    shifted = jnp.pad(offsets.astype(jnp.float32), ((0, 0), (0, 0), (3, 1)))
-    spread_offsets = jnp.repeat(shifted, PATCH, axis=2)
-    scratch = [
+def working_scratch(node_rows, width):
+    return [
         pltpu.VMEM((2, 2, node_rows * HALF, width), jnp.bfloat16),
         pltpu.VMEM((2, node_rows, width), jnp.float32),
         pltpu.VMEM((2, node_rows, width), jnp.float32),
     ]
+
+
+def match_pair(own, nodes, counts):
+    node_cols = nodes.shape[2]
+    node_rows = nodes.shape[1] // 2
+    width = own.shape[1] + 2 * BLOCK
+    blocks = width // BLOCK - 2
+    four = np.zeros((LANES, 4, PATCH))
+    for node in range(4):
+        four[node, node] = 1.0
+    constants = [jnp.asarray(t) for t in (bf16(four.reshape(LANES, BLOCK)),) + tables()]
+    laid = jnp.pad(nodes, ((0, 0), (0, 0), (ITERS, LANES - ITERS - node_cols)))
     vmem = pl.BlockSpec(memory_space=pltpu.VMEM)
-    specs = [vmem] * (2 + len(constants))
-    if counts is None:
-        body = functools.partial(plain_kernel, node_rows)
-        params = pltpu.CompilerParams(vmem_limit_bytes=56 * 1024 * 1024)
-    else:
-        body = functools.partial(pair_kernel, counts, node_rows)
-        params = pltpu.CompilerParams(
+    dma = pltpu.SemaphoreType.DMA
+    f32 = jnp.float32
+    out = pl.pallas_call(
+        functools.partial(pair_kernel, counts, node_rows, node_cols),
+        out_shape=jax.ShapeDtypeStruct((2, 2, 2 * node_rows, LANES), f32),
+        in_specs=[pl.BlockSpec(memory_space=pl.ANY)] + [vmem] * (1 + len(constants)),
+        out_specs=vmem,
+        scratch_shapes=working_scratch(node_rows, width)
+        + [
+            pltpu.VMEM((2, (node_rows + 1) * SPACING, width), jnp.bfloat16),
+            pltpu.VMEM((3, node_rows, LANES), f32),
+            pltpu.VMEM((3, node_rows, LANES), f32),
+            pltpu.VMEM((2, 3, 3, 4 * node_rows, LANES), f32),
+            pltpu.VMEM((3, 3, 4 * node_rows, LANES), f32),
+            dma,
+            dma((12,)),
+            dma((12,)),
+            dma((blocks,)),
+            dma((blocks,)),
+            dma,
+            dma((17,)),
+            dma((17,)),
+            dma((12,)),
+            dma((12,)),
+        ],
+        compiler_params=pltpu.CompilerParams(
             vmem_limit_bytes=56 * 1024 * 1024, collective_id=0, has_side_effects=True
-        )
-        specs[0] = pl.BlockSpec(memory_space=pl.ANY)
-        blocks = width // BLOCK - 2
-        scratch += [
-            pltpu.VMEM((2, (node_rows + 1) * SPACING, width), jnp.bfloat16),
-            pltpu.SemaphoreType.DMA,
-            pltpu.SemaphoreType.DMA((12,)),
-            pltpu.SemaphoreType.DMA((12,)),
-            pltpu.SemaphoreType.DMA((blocks,)),
-            pltpu.SemaphoreType.DMA((blocks,)),
-        ]
+        ),
+    )(own, laid, *constants)
+    out = out[..., ITERS : ITERS + node_cols]
+    return out[0], out[1]
+
+
+def match(strips, offsets):
+    node_rows, node_cols = offsets.shape[1:]
+    groups = node_cols // 4 + 1
+    constants = [jnp.asarray(table) for table in tables()]
+    shifted = jnp.pad(offsets.astype(jnp.float32), ((0, 0), (0, 0), (3, 1)))
+    spread_offsets = jnp.repeat(shifted, PATCH, axis=2)
+    vmem = pl.BlockSpec(memory_space=pltpu.VMEM)
     out = pl.pallas_call(
-        body,
+        functools.partial(plain_kernel, node_rows),
         out_shape=jax.ShapeDtypeStruct((groups, node_rows, 128), jnp.float32),
-        in_specs=specs,
+        in_specs=[vmem] * (2 + len(constants)),
         out_specs=vmem,
-        scratch_shapes=scratch,
-        compiler_params=params,
-    )(pixels, spread_offsets, *constants)
+        scratch_shapes=working_scratch(node_rows, strips.shape[2]),
+        compiler_params=pltpu.CompilerParams(vmem_limit_bytes=56 * 1024 * 1024),
+    )(strips, spread_offsets, *constants)
     sums = jnp.transpose(out[:, :, :12].reshape(groups, node_rows, 3, 4), (2, 1, 0, 3))
     sums = sums.reshape(3, node_rows, 4 * groups)[:, :, 3:-1]
     return jnp.stack([sums[2] / sums[0], sums[1] / sums[0], sums[0]], 0)
@@ -420,34 +628,19 @@
     pixel_rows, pixel_cols = own.shape
     node_rows = pixel_rows // SPACING
     slabs = lax.axis_size("gz")
-    place = lax.axis_index("gz")
     offsets = peak_offsets[:, 0].astype(jnp.float32)
     living = tissue.astype(jnp.float32)
     per_node = jnp.float32((2 * REACH + 1) ** 2)
 
-    if slabs == 2 and node_rows % 16 == 0 and pixel_cols % BLOCK == 0:
-        half_rows = node_rows // 2
-        swap = [(0, 1), (1, 0)]
-        first = place == 0
-        nodes = jnp.concatenate([offsets, living], 0)
-        other_nodes = lax.ppermute(nodes, "gz", swap)
-        nodes_0 = jnp.where(first, nodes, other_nodes)
-        nodes_1 = jnp.where(first, other_nodes, nodes)
+    if (
+        slabs == 2
+        and node_rows % 16 == 0
+        and pixel_cols % BLOCK == 0
+        and pixel_cols // SPACING + 2 * ITERS <= LANES
+    ):
         counts = tuple(lax.axis_size(axis) for axis in ("gz", "gx", "gy"))
-        ours = match(
-            own, lax.dynamic_slice_in_dim(nodes_0[:2], place * half_rows, half_rows, 1), counts
-        )
-        others = lax.ppermute(ours, "gz", swap)
-        matched = jnp.concatenate(
-            [jnp.where(first, ours, others), jnp.where(first, others, ours)], 1
-        )
-        target = jnp.stack([matched[:2], nodes_1[:2]], 1)
-        alive = jnp.stack([nodes_0[2], nodes_1[2]], 0)
-        stiffness = jnp.stack([nodes_0[2] * matched[2] / per_node, nodes_1[2]], 0)
-        moved = relax(target, stiffness, alive)
-        relaxed = jnp.where(first, moved[:, 0], moved[:, 1])
-        placed = jnp.where(first, moved[:, 0], moved[:, 0] + moved[:, 1])
-        return relaxed[:, None], placed[:, None]
+        moved, placed = match_pair(own, jnp.concatenate([offsets, living], 0), counts)
+        return moved[:, None], placed[:, None]
 
     before, after = bordered(own, "gx", 1, LANES)
     own = jnp.concatenate([before, own, after], 1)

time: 76.7 us -> 56.6 us (0.74)
  starting transfers between devices: 15.6 us -> 0 us
  waiting for transfers between devices: 10.5 us -> 0 us
  Pallas kernels: 43.1 us -> 52 us
  other arithmetic: 3.58 us -> 2.11 us
  local copies, waits for them, and re-layouts: 2.73 us -> 1.43 us
    ppermute x6 -> x0, starting transfers between devices: 15.6 us -> none  [the longest x4 13.5 us: beside(): return lax.ppermute(value, axis, pairs)]
    ppermute x6 -> x0, waiting for transfers between devices: 10.5 us -> none  [the longest x4 6.73 us: beside(): return lax.ppermute(value, axis, pairs)]
    pallas_call x1, Pallas kernels: 43.1 us -> 52 us  [match_pair(): pl.pallas_call(functools.partial(pair_kernel, counts, node_rows, node_col...]
    unnamed x4 -> x1, local copies, waits for them, and re-layouts: 0.07 us -> 1.43 us
    slice x7 -> x0, local copies, waits for them, and re-layouts: 1.17 us -> none  [the longest x1 1.01 us: match(): out[:, :, :12].reshape(groups, node_rows, 3, 4)]
    reshape x2 -> x0, local copies, waits for them, and re-layouts: 0.93 us -> none  [the longest x1 0.88 us: match(): spread_offsets = jnp.repeat(shifted, PATCH, axis=2)]
  transfers between devices with their start and end apart: 6 -> 0, of which waited for: 4 -> 0; matrix products, arithmetic and copies ran while one was open for 0% -> 0% of each run, Pallas kernels for 0% -> 0%
where the time goes in v3:
time: 56.6 us; the launch traced here: 56.2 us
  Pallas kernels  52 us (92%)
  other arithmetic  2.11 us (4%)
  local copies, waits for them, and re-layouts  1.43 us (3%)
  between operations  0.64 us (1%)
    pallas_call x1, Pallas kernels, match_pair(): pl.pallas_call(functools.partial(pair_kernel, counts, node_rows, node_col...  52 us
    unnamed x1, local copies, waits for them, and re-layouts  1.43 us

profile of v3, /device:TPU:1, one launch (start us, length us, event | category | flops | bytes accessed | tf_op | source)
XLA Modules:
  0.0 56.2 jit_solution(13331808983254563763)
XLA Ops:
  0.6 0.7 %convert_element_type.13 = f32[1,16,64]{2,1,0:T(8,128)S(1)} convert(s32[1,16,64]{2,1,0:T(8,128)} %param.12) | non-fusion elementwise | flops 1024 | bytes 8192 | tf_op jit(solution)/shard_map/convert_element_type | solution.py:632
  1.3 0.7 %fusion.1 = f32[2,16,64]{2,1,0:T(8,128)S(1)} fusion(s32[2,1,16,64]{3,2,1,0:T(8,128)} %param.13), kind=kLoop, calls=%fused_computation.5 | loop fusion | flops 2048 | bytes 16384 | tf_op jit(solution)/shard_map/convert_element_type | solution.py:631
  2.0 0.7 %select_maximum_fusion.nodes_ref = f32[3,16,128]{2,1,0:T(8,128)} fusion(f32[1,16,64]{2,1,0:T(8,128)S(1)} %convert_element_type.13, f32[2,16,64]{2,1,0:T(8,128)S(1)} %fusion.1), kind=kLoop, calls=%fused_computation.2 | loop fusion | flops 36864 | bytes 36864 | tf_op jit(solution)/shard_map/concatenate | solution.py:642
  2.7 52.0 %shard_map.122 = f32[2,2,16,128]{3,2,1,0:T(8,128)} custom-call(bf16[512,2048]{1,0:T(8,128)(2,1)} %bitcast.15, f32[3,16,128]{2,1,0:T(8,128)} %select_maximum_fusion.nodes_ref, bf16[128,256]{1,0:T(8,128)(2,1)} %constant.19.clone.four_ref, bf16[80,64]{1,0:T(8,128)(2,1)} %constant.20.clone.refs_0_, bf16[2,256,512]{2,1,0:T(8,128)(2,1)} %constant.21.clone.refs_1_, ...), custom_call_target="tpu_custom_call" | custom-call | tf_op jit(solution)/shard_map/pallas_call | solution.py:533
  54.8 1.4 %slice_bitcast_fusion = (f32[2,1,16,64]{3,2,1,0:T(8,128)}, f32[2,1,16,64]{3,2,1,0:T(8,128)}) fusion(f32[2,2,16,128]{3,2,1,0:T(8,128)} %shard_map.122), kind=kLoop, calls=%fused_computation.6 | loop fusion | bytes 32768

commit v4 on v3

--- a/solution.py
+++ b/solution.py
@@ -72,20 +72,19 @@
     rows[: lags.size, HALF:] = -fold * lag_sin[:HALF].T
     row_high, row_low = split(rows)
     row_back = np.concatenate([row_high, row_high, row_low], 1)
-    gather = np.zeros((2, 4, PATCH, 128))
+    gather = np.zeros((4, PATCH, 128))
     lane_lag = np.arange(PATCH) - FAR
     for node in range(4):
-        gather[0, node, :, node] = 1.0
-        gather[0, node, :, 4 + node] = lane_lag
-        gather[1, node, :, 8 + node] = 1.0
+        gather[node, :, node] = 1.0
+        gather[node, :, 4 + node] = lane_lag
     return (
         bf16(row_table),
         bf16(second.reshape(2, 256, 512)),
-        np.asarray(spread.reshape(256, 256), np.float32),
+        bf16(spread.reshape(256, 256)),
         back_high,
         back_low,
         row_back,
-        np.asarray(gather.reshape(2, 256, 128), np.float32),
+        bf16(gather.reshape(256, 128)),
     )
 
 
@@ -112,8 +111,18 @@
     def dot(a, b):
         return jnp.dot(a, b, preferred_element_type=f32)
 
-    def exact(a, b):
-        return jnp.dot(a, b, preferred_element_type=f32, precision=lax.Precision.HIGHEST)
+    def parts(value):
+        high = value.astype(b16)
+        rest = value - high.astype(f32)
+        middle = rest.astype(b16)
+        return [high.astype(f32), middle.astype(f32), rest - middle.astype(f32)]
+
+    def exact_pair(first, then, table):
+        stacked = jnp.concatenate(parts(first) + parts(then), 0).astype(b16)
+        got = dot(stacked, table)
+        n = first.shape[0]
+        terms = [got[k * n : (k + 1) * n] for k in range(6)]
+        return terms[0] + terms[1] + terms[2], terms[3] + terms[4] + terms[5]
 
     def over_rows(block):
         lanes = pl.ds(pl.multiple_of(block * BLOCK, BLOCK), BLOCK)
@@ -135,29 +144,40 @@
     row_lag = row_lag.astype(f32)
     col_lag = col_lag.astype(f32)
 
-    def over_columns(first, then, pair):
+    def crossed(first, then, pair):
         real, imag = slice(256 * pair, 256 * pair + 128), slice(256 * pair + 128, 256 * pair + 256)
         cross_real = first[:, real] * then[:, real] + first[:, imag] * then[:, imag]
         cross_imag = first[:, real] * then[:, imag] - first[:, imag] * then[:, real]
-        cross = jnp.concatenate([cross_real, cross_imag], 1)
+        return jnp.concatenate([cross_real, cross_imag], 1)
+
+    def over_columns(cross):
         high = cross.astype(b16)
         low = (cross - high.astype(f32)).astype(b16)
         return dot(high, back_high_ref[...]) + dot(low, back_high_ref[...]) + dot(high, back_low_ref[...])
 
     def four_columns(group):
         lanes = pl.ds(pl.multiple_of((group + 1) * LANES, LANES), BLOCK)
-        spectra, edges, energies = [], [], []
+        spectra = []
         for which in range(2):
             spectra.append(
                 dot(half_ref[which, 0, :, lanes], second_ref[0])
                 + dot(half_ref[which, 1, :, lanes], second_ref[1])
             )
-            edges.append(dot(nyquist_ref[which, :, lanes].astype(b16), second_ref[0]))
-            energies.append(exact(squares_ref[which, :, lanes], spread_ref[...]))
+        both = jnp.concatenate([nyquist_ref[0, :, lanes], nyquist_ref[1, :, lanes]], 0)
+        edges = dot(both.astype(b16), second_ref[0])
+        energies = exact_pair(squares_ref[0, :, lanes], squares_ref[1, :, lanes], spread_ref[...])
         scale = (sharpness / (PATCH * PATCH)) / jnp.sqrt(energies[0] * energies[1] + tiny_energy)
-        columns = [over_columns(spectra[0], spectra[1], pair) for pair in range(2)]
+        main = node_rows * HALF
+        back = over_columns(
+            jnp.concatenate(
+                [crossed(spectra[0], spectra[1], pair) for pair in range(2)]
+                + [crossed(edges[:node_rows], edges[node_rows:], pair) for pair in range(2)],
+                0,
+            )
+        )
+        columns = [back[:main], back[main : 2 * main]]
         edge_columns = jnp.concatenate(
-            [over_columns(edges[0], edges[1], pair)[:, :128] for pair in range(2)], 1
+            [back[2 * main : 2 * main + node_rows, :128], back[2 * main + node_rows :, :128]], 1
         )
         row_offset, col_offset = offsets_of(group)
         totals, row_totals = [], []
@@ -180,8 +200,11 @@
             weights = jnp.where(inside, jnp.exp(found * scale[i : i + 1]), 0.0)
             totals.append(jnp.sum(weights, axis=0, keepdims=True))
             row_totals.append(jnp.sum(weights * row_lag, axis=0, keepdims=True))
-        sums = exact(jnp.concatenate(totals, 0), gather_ref[0])
-        give(group, sums + exact(jnp.concatenate(row_totals, 0), gather_ref[1]))
+        plain, by_row = exact_pair(
+            jnp.concatenate(totals, 0), jnp.concatenate(row_totals, 0), gather_ref[...]
+        )
+        few = lax.broadcasted_iota(jnp.int32, (node_rows, LANES), 1)
+        give(group, plain + pltpu.roll(jnp.where(few < 4, by_row, 0.0), 8, 1))
 
     over_rows(0)
 

time: 56.6 us -> 54.5 us (0.963)
  Pallas kernels: 52 us -> 49.9 us
    pallas_call x1, Pallas kernels: 52 us -> 49.9 us  [match_pair(): pl.pallas_call(functools.partial(pair_kernel, counts, node_rows, node_col...]
where the time goes in v4:
time: 54.5 us; the launch traced here: 54.1 us
  Pallas kernels  49.9 us (92%)
  other arithmetic  2.11 us (4%)
  local copies, waits for them, and re-layouts  1.43 us (3%)
  between operations  0.64 us (1%)
    pallas_call x1, Pallas kernels, match_pair(): pl.pallas_call(functools.partial(pair_kernel, counts, node_rows, node_col...  49.9 us
    unnamed x1, local copies, waits for them, and re-layouts  1.43 us

profile of v4, /device:TPU:1, one launch (start us, length us, event | category | flops | bytes accessed | tf_op | source)
XLA Modules:
  0.0 54.1 jit_solution(12931665829729032774)
XLA Ops:
  0.6 0.7 %convert_element_type.13 = f32[1,16,64]{2,1,0:T(8,128)S(1)} convert(s32[1,16,64]{2,1,0:T(8,128)} %param.12) | non-fusion elementwise | flops 1024 | bytes 8192 | tf_op jit(solution)/shard_map/convert_element_type | solution.py:655
  1.3 0.7 %fusion.1 = f32[2,16,64]{2,1,0:T(8,128)S(1)} fusion(s32[2,1,16,64]{3,2,1,0:T(8,128)} %param.13), kind=kLoop, calls=%fused_computation.5 | loop fusion | flops 2048 | bytes 16384 | tf_op jit(solution)/shard_map/convert_element_type | solution.py:654
  2.0 0.7 %select_maximum_fusion.nodes_ref = f32[3,16,128]{2,1,0:T(8,128)} fusion(f32[1,16,64]{2,1,0:T(8,128)S(1)} %convert_element_type.13, f32[2,16,64]{2,1,0:T(8,128)S(1)} %fusion.1), kind=kLoop, calls=%fused_computation.2 | loop fusion | flops 36864 | bytes 36864 | tf_op jit(solution)/shard_map/concatenate | solution.py:665
  2.7 49.9 %shard_map.122 = f32[2,2,16,128]{3,2,1,0:T(8,128)} custom-call(bf16[512,2048]{1,0:T(8,128)(2,1)} %bitcast.15, f32[3,16,128]{2,1,0:T(8,128)} %select_maximum_fusion.nodes_ref, bf16[128,256]{1,0:T(8,128)(2,1)} %constant.19.clone.four_ref, bf16[80,64]{1,0:T(8,128)(2,1)} %constant.20.clone.refs_0_, bf16[2,256,512]{2,1,0:T(8,128)(2,1)} %constant.21.clone.refs_1_, ...), custom_call_target="tpu_custom_call" | custom-call | tf_op jit(solution)/shard_map/pallas_call | solution.py:556
  52.7 1.4 %slice_bitcast_fusion = (f32[2,1,16,64]{3,2,1,0:T(8,128)}, f32[2,1,16,64]{3,2,1,0:T(8,128)}) fusion(f32[2,2,16,128]{3,2,1,0:T(8,128)} %shard_map.122), kind=kLoop, calls=%fused_computation.6 | loop fusion | bytes 32768

commit v5 on v4

--- a/solution.py
+++ b/solution.py
@@ -194,12 +194,13 @@
             low = (field - high.astype(f32)).astype(b16)
             found = dot(row_back_ref[...], jnp.concatenate([high, low, high], 0))
             found = found + alternate * edge_columns[i : i + 1]
-            inside = (jnp.abs(row_lag - row_offset[i : i + 1]) <= REACH) & (
-                jnp.abs(col_lag - col_offset[i : i + 1]) <= REACH
+            in_rows = jnp.abs(row_lag - row_offset[i : i + 1]) <= REACH
+            in_cols = jnp.abs(col_lag[:1] - col_offset[i : i + 1]) <= REACH
+            weights = jnp.where(in_rows, jnp.exp(found * scale[i : i + 1]), 0.0)
+            totals.append(jnp.where(in_cols, jnp.sum(weights, axis=0, keepdims=True), 0.0))
+            row_totals.append(
+                jnp.where(in_cols, jnp.sum(weights * row_lag, axis=0, keepdims=True), 0.0)
             )
-            weights = jnp.where(inside, jnp.exp(found * scale[i : i + 1]), 0.0)
-            totals.append(jnp.sum(weights, axis=0, keepdims=True))
-            row_totals.append(jnp.sum(weights * row_lag, axis=0, keepdims=True))
         plain, by_row = exact_pair(
             jnp.concatenate(totals, 0), jnp.concatenate(row_totals, 0), gather_ref[...]
         )

time: 54.5 us -> 54.4 us (level)
  no operation moved by 1% of the time
where the time goes in v5:
time: 54.4 us; the launch traced here: 54 us
  Pallas kernels  49.8 us (92%)
  other arithmetic  2.11 us (4%)
  local copies, waits for them, and re-layouts  1.43 us (3%)
  between operations  0.64 us (1%)
    pallas_call x1, Pallas kernels, match_pair(): pl.pallas_call(functools.partial(pair_kernel, counts, node_rows, node_col...  49.8 us
    unnamed x1, local copies, waits for them, and re-layouts  1.43 us

profile of v5, /device:TPU:1, one launch (start us, length us, event | category | flops | bytes accessed | tf_op | source)
XLA Modules:
  0.0 54.0 jit_solution(7789647245446594111)
XLA Ops:
  0.6 0.7 %convert_element_type.13 = f32[1,16,64]{2,1,0:T(8,128)S(1)} convert(s32[1,16,64]{2,1,0:T(8,128)} %param.12) | non-fusion elementwise | flops 1024 | bytes 8192 | tf_op jit(solution)/shard_map/convert_element_type | solution.py:656
  1.3 0.7 %fusion.1 = f32[2,16,64]{2,1,0:T(8,128)S(1)} fusion(s32[2,1,16,64]{3,2,1,0:T(8,128)} %param.13), kind=kLoop, calls=%fused_computation.5 | loop fusion | flops 2048 | bytes 16384 | tf_op jit(solution)/shard_map/convert_element_type | solution.py:655
  2.0 0.7 %select_maximum_fusion.nodes_ref = f32[3,16,128]{2,1,0:T(8,128)} fusion(f32[1,16,64]{2,1,0:T(8,128)S(1)} %convert_element_type.13, f32[2,16,64]{2,1,0:T(8,128)S(1)} %fusion.1), kind=kLoop, calls=%fused_computation.2 | loop fusion | flops 36864 | bytes 36864 | tf_op jit(solution)/shard_map/concatenate | solution.py:666
  2.7 49.8 %shard_map.122 = f32[2,2,16,128]{3,2,1,0:T(8,128)} custom-call(bf16[512,2048]{1,0:T(8,128)(2,1)} %bitcast.15, f32[3,16,128]{2,1,0:T(8,128)} %select_maximum_fusion.nodes_ref, bf16[128,256]{1,0:T(8,128)(2,1)} %constant.19.clone.four_ref, bf16[80,64]{1,0:T(8,128)(2,1)} %constant.20.clone.refs_0_, bf16[2,256,512]{2,1,0:T(8,128)(2,1)} %constant.21.clone.refs_1_, ...), custom_call_target="tpu_custom_call" | custom-call | tf_op jit(solution)/shard_map/pallas_call | solution.py:557
  52.5 1.4 %slice_bitcast_fusion = (f32[2,1,16,64]{3,2,1,0:T(8,128)}, f32[2,1,16,64]{3,2,1,0:T(8,128)}) fusion(f32[2,2,16,128]{3,2,1,0:T(8,128)} %shard_map.122), kind=kLoop, calls=%fused_computation.6 | loop fusion | bytes 32768
